TPU v7x, 128 devices: a whole 4x4x4 slice. The times are simulated.
128 devices in a mesh: ctx: 32 (over x, y, core), head: 4 (over z).
Axes of the slice: x: 4, y: 4, z: 4, core: 2. Of those that a mesh axis runs over, the one named last changes fastest.
Arguments:
- queries: bfloat16 [32768, 2048], P('ctx', 'head'), may hold values from -80 to 80
- row_keys: bfloat16 [32768, 128], P('ctx'), may hold values from -4 to 4
- row_values: bfloat16 [32768, 128], P('ctx'), may hold values from -12 to 12
- cached_keys: bfloat16 [4096, 128], P('ctx'), may hold values from -4 to 4
- cached_values: bfloat16 [4096, 128], P('ctx'), may hold values from -12 to 12
- doc_ids: int32 [32768], replicated, may hold values from 0 to 31, never falling along the last dimension, each value on 1 to 4096 neighbouring positions
- prefix_lens: int32 [32], replicated, may hold values from 1 to 512, 4096 in all
- block_order: int32 [256], replicated, may hold values from 0 to 255, each once
- out_weight: bfloat16 [2048, 4096], P('head'), may hold values from -0.25 to 0.25
Outputs:
- mixed: bfloat16 [32768, 4096], P('ctx', 'head')
Inputs may be any that keep to these rules, and one draw needn't show every extreme that they name: `doc_ids`: row positions in row order; numbers never fall; each document has 1 to 4096 positions. `prefix_lens`: the lengths sum to 4096; cached rows hold the documents' prefixes in document order. `block_order`: each row block stands in exactly one slot block.
All inputs are finite; a program needn't handle non-finite values.
Results may differ from a plain program's by a relative error of at most 0.017.
Values may be sent and summed in bfloat16 or wider, within the bound.
No kernel may reach another device: no remote copies, remote signals or barrier semaphores. Data moves between devices by JAX's collectives and lax.ppermute only.
A program may use at most 128 MiB of HBM per device.

v0:
```python
import jax
import jax.numpy as jnp
from jax import lax
from jax.sharding import PartitionSpec as P

BLK = 128


NEG = -1e30


def on_device(
    queries,
    row_keys,
    row_values,
    cached_keys,
    cached_values,
    doc_ids,
    prefix_lens,
    block_order,
    out_weight,
):
    local_rows = queries.shape[0]
    head_size = row_keys.shape[1]
    local_heads = queries.shape[1] // head_size
    all_rows = doc_ids.shape[0]
    block_count = block_order.shape[0]
    scale = 1.0 / head_size**0.5
    shard_index = lax.axis_index("ctx")
    inside = jnp.arange(BLK, dtype=jnp.int32)
    slot_pos = (block_order[:, None] * BLK + inside[None, :]).reshape(all_rows)
    slot_doc = doc_ids.reshape(block_count, BLK)[block_order].reshape(all_rows)
    query_pos = lax.dynamic_slice_in_dim(slot_pos, shard_index * local_rows, local_rows, 0)
    query_doc = lax.dynamic_slice_in_dim(slot_doc, shard_index * local_rows, local_rows, 0)
    query_three = queries.reshape(local_rows, local_heads, head_size)
    prefix_end = jnp.cumsum(prefix_lens)
    cached_rows = cached_keys.shape[0] * lax.axis_size("ctx")
    cached_index = jnp.arange(cached_rows, dtype=jnp.int32)
    cached_doc_all = jnp.sum(
        (prefix_end[None, :] <= cached_index[:, None]).astype(jnp.int32), axis=1
    )

    def update(carry, key_block, value_block, key_mask):
        running_top, running_total, running_sum = carry
        score = (
            jnp.einsum("qhd,kd->hqk", query_three, key_block, preferred_element_type=jnp.float32)
            * scale
        )
        score = jnp.where(key_mask[None], score, NEG)
        new_top = jnp.maximum(running_top, jnp.max(score, axis=-1))
        factor = jnp.exp(running_top - new_top)
        weight = jnp.where(key_mask[None], jnp.exp(score - new_top[..., None]), 0.0)
        new_total = running_total * factor + jnp.sum(weight, axis=-1)
        product = jnp.einsum(
            "hqk,kd->hqd",
            weight.astype(jnp.bfloat16),
            value_block,
            preferred_element_type=jnp.float32,
        )
        return (new_top, new_total, running_sum * factor[..., None] + product)

    def attend(carry, key_block, value_block, key_mask):
        return lax.cond(
            jnp.any(key_mask),
            lambda state: update(state, key_block, value_block, key_mask),
            lambda state: state,
            carry,
        )

    def sweep(carry, key_piece, value_piece, masker):
        count = key_piece.shape[0]
        width = 512

        def one_step(step_index, state):
            key_block = lax.dynamic_slice_in_dim(key_piece, step_index * width, width, 0)
            value_block = lax.dynamic_slice_in_dim(value_piece, step_index * width, width, 0)
            return attend(state, key_block, value_block, masker(step_index * width, width))

        return lax.fori_loop(0, count // width, one_step, carry)

    def row_mask(begin, width):
        key_pos = lax.dynamic_slice_in_dim(slot_pos, begin, width, 0)
        key_doc = lax.dynamic_slice_in_dim(slot_doc, begin, width, 0)
        return (key_doc[None, :] == query_doc[:, None]) & (key_pos[None, :] <= query_pos[:, None])

    def cached_mask(begin, width):
        cached_doc = lax.dynamic_slice_in_dim(cached_doc_all, begin, width, 0)
        return cached_doc[None, :] == query_doc[:, None]

    initial = (
        jnp.full((local_heads, local_rows), NEG, jnp.float32),
        jnp.zeros((local_heads, local_rows), jnp.float32),
        jnp.zeros((local_heads, local_rows, head_size), jnp.float32),
    )
    pieces = (
        lax.all_gather(row_keys, "ctx", axis=0, tiled=True),
        lax.all_gather(row_values, "ctx", axis=0, tiled=True),
    )
    carry = sweep(initial, pieces[0], pieces[1], row_mask)
    pieces = (
        lax.all_gather(cached_keys, "ctx", axis=0, tiled=True),
        lax.all_gather(cached_values, "ctx", axis=0, tiled=True),
    )
    carry = sweep(carry, pieces[0], pieces[1], cached_mask)
    final_total = carry[1]
    final_sum = carry[2]
    attended = final_sum / final_total[..., None]
    attended = (
        jnp.transpose(attended, (1, 0, 2))
        .reshape(local_rows, local_heads * head_size)
        .astype(jnp.bfloat16)
    )
    partial_term = jnp.dot(attended, out_weight, preferred_element_type=jnp.float32)
    return lax.psum_scatter(
        partial_term.astype(jnp.bfloat16), "head", scatter_dimension=1, tiled=True
    )


def solution(mesh):
    placed = (
        P("ctx", "head"),
        P("ctx", None),
        P("ctx", None),
        P("ctx", None),
        P("ctx", None),
        P(),
        P(),
        P(),
        P("head", None),
    )
    return jax.shard_map(
        on_device, mesh=mesh, in_specs=placed, out_specs=P("ctx", "head"), check_vma=False
    )
```

profile of v0, /device:TPU:1, one launch (start us, length us, event | category | flops | bytes accessed | tf_op | source)
XLA Modules:
  0.0 1030.6 jit_solution(12605433742025179641)
XLA Ops:
  14.2 51.8 %all-gather.5.cloned.1.call-done = bf16[32768,128]{1,0:T(8,128)(2,1)} async-done(((bf16[1024,128]{1,0:T(8,128)(2,1)}), bf16[32768,128]{1,0:T(8,128)(2,1)}) %all-gather.5.cloned.1.call-update) | async-done | bytes 8388624 | tf_op jit(solution)/shard_map/all_gather | solution.py:96
  66.1 54.7 %all-gather.7.cloned.1.call-done = bf16[32768,128]{1,0:T(8,128)(2,1)} async-done(((bf16[1024,128]{1,0:T(8,128)(2,1)}), bf16[32768,128]{1,0:T(8,128)(2,1)}) %all-gather.7.cloned.1.call-update) | async-done | bytes 8388624 | tf_op jit(solution)/shard_map/all_gather | solution.py:97
  122.2 592.4 %while.34 = (s32[]{:T(128)}, f32[4,1024]{1,0:T(4,128)S(1)}, f32[4,1024]{1,0:T(4,128)S(1)}, f32[4,1024,128]{2,1,0:T(8,128)}, s32[32768]{0:T(1024)S(1)}, /*index=5...) while((s32[]{:T(128)}, f32[4,1024]{1,0:T(4,128)S(1)}, ...), condition=%wide.region_6.7_spmd, body=%wide.region_0.6_spmd.sunk | while | flops 1104158720 | bytes 49829240 | solution.py:79
  128.7 10.3 %conditional.4 = ((f32[4,1024]{1,0:T(4,128)S(1)}, f32[4,1024]{1,0:T(4,128)S(1)}, f32[4,1024,128]{2,1,0:T(8,128)})) conditional(s32[]{:T(128)} %convert_element_type.57, (f32[4,1024]{1,0:T(4,128)S(1)}, f32[4,1024]{1,0:T(4,128)S(1)}, f32[4,1024,128]{2,1,0:T(8,128)}) %tuple.90, (pred[1024,512]{0,1:T(8,128)(4,1)S(1)}, bf16[32768,128]{1,0:T(8,128)(2,1)}, ...), branch_computations={%region_2.2_spmd, %region_3.0_spmd} | conditional | flops 1102061568 | bytes 49284184 | solution.py:63
  141.2 10.3 %conditional.4 = ((f32[4,1024]{1,0:T(4,128)S(1)}, f32[4,1024]{1,0:T(4,128)S(1)}, f32[4,1024,128]{2,1,0:T(8,128)})) conditional(s32[]{:T(128)} %convert_element_type.57, (f32[4,1024]{1,0:T(4,128)S(1)}, f32[4,1024]{1,0:T(4,128)S(1)}, f32[4,1024,128]{2,1,0:T(8,128)}) %tuple.90, (pred[1024,512]{0,1:T(8,128)(4,1)S(1)}, bf16[32768,128]{1,0:T(8,128)(2,1)}, ...), branch_computations={%region_2.2_spmd, %region_3.0_spmd} | conditional | flops 1102061568 | bytes 49284184 | solution.py:63
  153.7 10.3 %conditional.4 = ((f32[4,1024]{1,0:T(4,128)S(1)}, f32[4,1024]{1,0:T(4,128)S(1)}, f32[4,1024,128]{2,1,0:T(8,128)})) conditional(s32[]{:T(128)} %convert_element_type.57, (f32[4,1024]{1,0:T(4,128)S(1)}, f32[4,1024]{1,0:T(4,128)S(1)}, f32[4,1024,128]{2,1,0:T(8,128)}) %tuple.90, (pred[1024,512]{0,1:T(8,128)(4,1)S(1)}, bf16[32768,128]{1,0:T(8,128)(2,1)}, ...), branch_computations={%region_2.2_spmd, %region_3.0_spmd} | conditional | flops 1102061568 | bytes 49284184 | solution.py:63
  166.1 10.3 %conditional.4 = ((f32[4,1024]{1,0:T(4,128)S(1)}, f32[4,1024]{1,0:T(4,128)S(1)}, f32[4,1024,128]{2,1,0:T(8,128)})) conditional(s32[]{:T(128)} %convert_element_type.57, (f32[4,1024]{1,0:T(4,128)S(1)}, f32[4,1024]{1,0:T(4,128)S(1)}, f32[4,1024,128]{2,1,0:T(8,128)}) %tuple.90, (pred[1024,512]{0,1:T(8,128)(4,1)S(1)}, bf16[32768,128]{1,0:T(8,128)(2,1)}, ...), branch_computations={%region_2.2_spmd, %region_3.0_spmd} | conditional | flops 1102061568 | bytes 49284184 | solution.py:63
  178.6 10.3 %conditional.4 = ((f32[4,1024]{1,0:T(4,128)S(1)}, f32[4,1024]{1,0:T(4,128)S(1)}, f32[4,1024,128]{2,1,0:T(8,128)})) conditional(s32[]{:T(128)} %convert_element_type.57, (f32[4,1024]{1,0:T(4,128)S(1)}, f32[4,1024]{1,0:T(4,128)S(1)}, f32[4,1024,128]{2,1,0:T(8,128)}) %tuple.90, (pred[1024,512]{0,1:T(8,128)(4,1)S(1)}, bf16[32768,128]{1,0:T(8,128)(2,1)}, ...), branch_computations={%region_2.2_spmd, %region_3.0_spmd} | conditional | flops 1102061568 | bytes 49284184 | solution.py:63
  191.1 10.3 %conditional.4 = ((f32[4,1024]{1,0:T(4,128)S(1)}, f32[4,1024]{1,0:T(4,128)S(1)}, f32[4,1024,128]{2,1,0:T(8,128)})) conditional(s32[]{:T(128)} %convert_element_type.57, (f32[4,1024]{1,0:T(4,128)S(1)}, f32[4,1024]{1,0:T(4,128)S(1)}, f32[4,1024,128]{2,1,0:T(8,128)}) %tuple.90, (pred[1024,512]{0,1:T(8,128)(4,1)S(1)}, bf16[32768,128]{1,0:T(8,128)(2,1)}, ...), branch_computations={%region_2.2_spmd, %region_3.0_spmd} | conditional | flops 1102061568 | bytes 49284184 | solution.py:63
  205.7 10.3 %conditional.4 = ((f32[4,1024]{1,0:T(4,128)S(1)}, f32[4,1024]{1,0:T(4,128)S(1)}, f32[4,1024,128]{2,1,0:T(8,128)})) conditional(s32[]{:T(128)} %convert_element_type.57, (f32[4,1024]{1,0:T(4,128)S(1)}, f32[4,1024]{1,0:T(4,128)S(1)}, f32[4,1024,128]{2,1,0:T(8,128)}) %tuple.90, (pred[1024,512]{0,1:T(8,128)(4,1)S(1)}, bf16[32768,128]{1,0:T(8,128)(2,1)}, ...), branch_computations={%region_2.2_spmd, %region_3.0_spmd} | conditional | flops 1102061568 | bytes 49284184 | solution.py:63
  218.2 10.3 %conditional.4 = ((f32[4,1024]{1,0:T(4,128)S(1)}, f32[4,1024]{1,0:T(4,128)S(1)}, f32[4,1024,128]{2,1,0:T(8,128)})) conditional(s32[]{:T(128)} %convert_element_type.57, (f32[4,1024]{1,0:T(4,128)S(1)}, f32[4,1024]{1,0:T(4,128)S(1)}, f32[4,1024,128]{2,1,0:T(8,128)}) %tuple.90, (pred[1024,512]{0,1:T(8,128)(4,1)S(1)}, bf16[32768,128]{1,0:T(8,128)(2,1)}, ...), branch_computations={%region_2.2_spmd, %region_3.0_spmd} | conditional | flops 1102061568 | bytes 49284184 | solution.py:63
  245.4 10.3 %conditional.4 = ((f32[4,1024]{1,0:T(4,128)S(1)}, f32[4,1024]{1,0:T(4,128)S(1)}, f32[4,1024,128]{2,1,0:T(8,128)})) conditional(s32[]{:T(128)} %convert_element_type.57, (f32[4,1024]{1,0:T(4,128)S(1)}, f32[4,1024]{1,0:T(4,128)S(1)}, f32[4,1024,128]{2,1,0:T(8,128)}) %tuple.90, (pred[1024,512]{0,1:T(8,128)(4,1)S(1)}, bf16[32768,128]{1,0:T(8,128)(2,1)}, ...), branch_computations={%region_2.2_spmd, %region_3.0_spmd} | conditional | flops 1102061568 | bytes 49284184 | solution.py:63
  260.0 10.3 %conditional.4 = ((f32[4,1024]{1,0:T(4,128)S(1)}, f32[4,1024]{1,0:T(4,128)S(1)}, f32[4,1024,128]{2,1,0:T(8,128)})) conditional(s32[]{:T(128)} %convert_element_type.57, (f32[4,1024]{1,0:T(4,128)S(1)}, f32[4,1024]{1,0:T(4,128)S(1)}, f32[4,1024,128]{2,1,0:T(8,128)}) %tuple.90, (pred[1024,512]{0,1:T(8,128)(4,1)S(1)}, bf16[32768,128]{1,0:T(8,128)(2,1)}, ...), branch_computations={%region_2.2_spmd, %region_3.0_spmd} | conditional | flops 1102061568 | bytes 49284184 | solution.py:63
  272.5 10.3 %conditional.4 = ((f32[4,1024]{1,0:T(4,128)S(1)}, f32[4,1024]{1,0:T(4,128)S(1)}, f32[4,1024,128]{2,1,0:T(8,128)})) conditional(s32[]{:T(128)} %convert_element_type.57, (f32[4,1024]{1,0:T(4,128)S(1)}, f32[4,1024]{1,0:T(4,128)S(1)}, f32[4,1024,128]{2,1,0:T(8,128)}) %tuple.90, (pred[1024,512]{0,1:T(8,128)(4,1)S(1)}, bf16[32768,128]{1,0:T(8,128)(2,1)}, ...), branch_computations={%region_2.2_spmd, %region_3.0_spmd} | conditional | flops 1102061568 | bytes 49284184 | solution.py:63
  284.9 10.3 %conditional.4 = ((f32[4,1024]{1,0:T(4,128)S(1)}, f32[4,1024]{1,0:T(4,128)S(1)}, f32[4,1024,128]{2,1,0:T(8,128)})) conditional(s32[]{:T(128)} %convert_element_type.57, (f32[4,1024]{1,0:T(4,128)S(1)}, f32[4,1024]{1,0:T(4,128)S(1)}, f32[4,1024,128]{2,1,0:T(8,128)}) %tuple.90, (pred[1024,512]{0,1:T(8,128)(4,1)S(1)}, bf16[32768,128]{1,0:T(8,128)(2,1)}, ...), branch_computations={%region_2.2_spmd, %region_3.0_spmd} | conditional | flops 1102061568 | bytes 49284184 | solution.py:63
  297.4 10.3 %conditional.4 = ((f32[4,1024]{1,0:T(4,128)S(1)}, f32[4,1024]{1,0:T(4,128)S(1)}, f32[4,1024,128]{2,1,0:T(8,128)})) conditional(s32[]{:T(128)} %convert_element_type.57, (f32[4,1024]{1,0:T(4,128)S(1)}, f32[4,1024]{1,0:T(4,128)S(1)}, f32[4,1024,128]{2,1,0:T(8,128)}) %tuple.90, (pred[1024,512]{0,1:T(8,128)(4,1)S(1)}, bf16[32768,128]{1,0:T(8,128)(2,1)}, ...), branch_computations={%region_2.2_spmd, %region_3.0_spmd} | conditional | flops 1102061568 | bytes 49284184 | solution.py:63
  309.9 10.3 %conditional.4 = ((f32[4,1024]{1,0:T(4,128)S(1)}, f32[4,1024]{1,0:T(4,128)S(1)}, f32[4,1024,128]{2,1,0:T(8,128)})) conditional(s32[]{:T(128)} %convert_element_type.57, (f32[4,1024]{1,0:T(4,128)S(1)}, f32[4,1024]{1,0:T(4,128)S(1)}, f32[4,1024,128]{2,1,0:T(8,128)}) %tuple.90, (pred[1024,512]{0,1:T(8,128)(4,1)S(1)}, bf16[32768,128]{1,0:T(8,128)(2,1)}, ...), branch_computations={%region_2.2_spmd, %region_3.0_spmd} | conditional | flops 1102061568 | bytes 49284184 | solution.py:63
  324.5 10.3 %conditional.4 = ((f32[4,1024]{1,0:T(4,128)S(1)}, f32[4,1024]{1,0:T(4,128)S(1)}, f32[4,1024,128]{2,1,0:T(8,128)})) conditional(s32[]{:T(128)} %convert_element_type.57, (f32[4,1024]{1,0:T(4,128)S(1)}, f32[4,1024]{1,0:T(4,128)S(1)}, f32[4,1024,128]{2,1,0:T(8,128)}) %tuple.90, (pred[1024,512]{0,1:T(8,128)(4,1)S(1)}, bf16[32768,128]{1,0:T(8,128)(2,1)}, ...), branch_computations={%region_2.2_spmd, %region_3.0_spmd} | conditional | flops 1102061568 | bytes 49284184 | solution.py:63
  337.0 10.3 %conditional.4 = ((f32[4,1024]{1,0:T(4,128)S(1)}, f32[4,1024]{1,0:T(4,128)S(1)}, f32[4,1024,128]{2,1,0:T(8,128)})) conditional(s32[]{:T(128)} %convert_element_type.57, (f32[4,1024]{1,0:T(4,128)S(1)}, f32[4,1024]{1,0:T(4,128)S(1)}, f32[4,1024,128]{2,1,0:T(8,128)}) %tuple.90, (pred[1024,512]{0,1:T(8,128)(4,1)S(1)}, bf16[32768,128]{1,0:T(8,128)(2,1)}, ...), branch_computations={%region_2.2_spmd, %region_3.0_spmd} | conditional | flops 1102061568 | bytes 49284184 | solution.py:63
  349.5 10.3 %conditional.4 = ((f32[4,1024]{1,0:T(4,128)S(1)}, f32[4,1024]{1,0:T(4,128)S(1)}, f32[4,1024,128]{2,1,0:T(8,128)})) conditional(s32[]{:T(128)} %convert_element_type.57, (f32[4,1024]{1,0:T(4,128)S(1)}, f32[4,1024]{1,0:T(4,128)S(1)}, f32[4,1024,128]{2,1,0:T(8,128)}) %tuple.90, (pred[1024,512]{0,1:T(8,128)(4,1)S(1)}, bf16[32768,128]{1,0:T(8,128)(2,1)}, ...), branch_computations={%region_2.2_spmd, %region_3.0_spmd} | conditional | flops 1102061568 | bytes 49284184 | solution.py:63
  361.9 10.3 %conditional.4 = ((f32[4,1024]{1,0:T(4,128)S(1)}, f32[4,1024]{1,0:T(4,128)S(1)}, f32[4,1024,128]{2,1,0:T(8,128)})) conditional(s32[]{:T(128)} %convert_element_type.57, (f32[4,1024]{1,0:T(4,128)S(1)}, f32[4,1024]{1,0:T(4,128)S(1)}, f32[4,1024,128]{2,1,0:T(8,128)}) %tuple.90, (pred[1024,512]{0,1:T(8,128)(4,1)S(1)}, bf16[32768,128]{1,0:T(8,128)(2,1)}, ...), branch_computations={%region_2.2_spmd, %region_3.0_spmd} | conditional | flops 1102061568 | bytes 49284184 | solution.py:63
  374.4 10.3 %conditional.4 = ((f32[4,1024]{1,0:T(4,128)S(1)}, f32[4,1024]{1,0:T(4,128)S(1)}, f32[4,1024,128]{2,1,0:T(8,128)})) conditional(s32[]{:T(128)} %convert_element_type.57, (f32[4,1024]{1,0:T(4,128)S(1)}, f32[4,1024]{1,0:T(4,128)S(1)}, f32[4,1024,128]{2,1,0:T(8,128)}) %tuple.90, (pred[1024,512]{0,1:T(8,128)(4,1)S(1)}, bf16[32768,128]{1,0:T(8,128)(2,1)}, ...), branch_computations={%region_2.2_spmd, %region_3.0_spmd} | conditional | flops 1102061568 | bytes 49284184 | solution.py:63
  386.8 10.3 %conditional.4 = ((f32[4,1024]{1,0:T(4,128)S(1)}, f32[4,1024]{1,0:T(4,128)S(1)}, f32[4,1024,128]{2,1,0:T(8,128)})) conditional(s32[]{:T(128)} %convert_element_type.57, (f32[4,1024]{1,0:T(4,128)S(1)}, f32[4,1024]{1,0:T(4,128)S(1)}, f32[4,1024,128]{2,1,0:T(8,128)}) %tuple.90, (pred[1024,512]{0,1:T(8,128)(4,1)S(1)}, bf16[32768,128]{1,0:T(8,128)(2,1)}, ...), branch_computations={%region_2.2_spmd, %region_3.0_spmd} | conditional | flops 1102061568 | bytes 49284184 | solution.py:63
  403.7 10.3 %conditional.4 = ((f32[4,1024]{1,0:T(4,128)S(1)}, f32[4,1024]{1,0:T(4,128)S(1)}, f32[4,1024,128]{2,1,0:T(8,128)})) conditional(s32[]{:T(128)} %convert_element_type.57, (f32[4,1024]{1,0:T(4,128)S(1)}, f32[4,1024]{1,0:T(4,128)S(1)}, f32[4,1024,128]{2,1,0:T(8,128)}) %tuple.90, (pred[1024,512]{0,1:T(8,128)(4,1)S(1)}, bf16[32768,128]{1,0:T(8,128)(2,1)}, ...), branch_computations={%region_2.2_spmd, %region_3.0_spmd} | conditional | flops 1102061568 | bytes 49284184 | solution.py:63
  416.2 10.3 %conditional.4 = ((f32[4,1024]{1,0:T(4,128)S(1)}, f32[4,1024]{1,0:T(4,128)S(1)}, f32[4,1024,128]{2,1,0:T(8,128)})) conditional(s32[]{:T(128)} %convert_element_type.57, (f32[4,1024]{1,0:T(4,128)S(1)}, f32[4,1024]{1,0:T(4,128)S(1)}, f32[4,1024,128]{2,1,0:T(8,128)}) %tuple.90, (pred[1024,512]{0,1:T(8,128)(4,1)S(1)}, bf16[32768,128]{1,0:T(8,128)(2,1)}, ...), branch_computations={%region_2.2_spmd, %region_3.0_spmd} | conditional | flops 1102061568 | bytes 49284184 | solution.py:63
  433.0 10.3 %conditional.4 = ((f32[4,1024]{1,0:T(4,128)S(1)}, f32[4,1024]{1,0:T(4,128)S(1)}, f32[4,1024,128]{2,1,0:T(8,128)})) conditional(s32[]{:T(128)} %convert_element_type.57, (f32[4,1024]{1,0:T(4,128)S(1)}, f32[4,1024]{1,0:T(4,128)S(1)}, f32[4,1024,128]{2,1,0:T(8,128)}) %tuple.90, (pred[1024,512]{0,1:T(8,128)(4,1)S(1)}, bf16[32768,128]{1,0:T(8,128)(2,1)}, ...), branch_computations={%region_2.2_spmd, %region_3.0_spmd} | conditional | flops 1102061568 | bytes 49284184 | solution.py:63
  447.7 10.3 %conditional.4 = ((f32[4,1024]{1,0:T(4,128)S(1)}, f32[4,1024]{1,0:T(4,128)S(1)}, f32[4,1024,128]{2,1,0:T(8,128)})) conditional(s32[]{:T(128)} %convert_element_type.57, (f32[4,1024]{1,0:T(4,128)S(1)}, f32[4,1024]{1,0:T(4,128)S(1)}, f32[4,1024,128]{2,1,0:T(8,128)}) %tuple.90, (pred[1024,512]{0,1:T(8,128)(4,1)S(1)}, bf16[32768,128]{1,0:T(8,128)(2,1)}, ...), branch_computations={%region_2.2_spmd, %region_3.0_spmd} | conditional | flops 1102061568 | bytes 49284184 | solution.py:63
  460.1 10.3 %conditional.4 = ((f32[4,1024]{1,0:T(4,128)S(1)}, f32[4,1024]{1,0:T(4,128)S(1)}, f32[4,1024,128]{2,1,0:T(8,128)})) conditional(s32[]{:T(128)} %convert_element_type.57, (f32[4,1024]{1,0:T(4,128)S(1)}, f32[4,1024]{1,0:T(4,128)S(1)}, f32[4,1024,128]{2,1,0:T(8,128)}) %tuple.90, (pred[1024,512]{0,1:T(8,128)(4,1)S(1)}, bf16[32768,128]{1,0:T(8,128)(2,1)}, ...), branch_computations={%region_2.2_spmd, %region_3.0_spmd} | conditional | flops 1102061568 | bytes 49284184 | solution.py:63
  474.8 10.3 %conditional.4 = ((f32[4,1024]{1,0:T(4,128)S(1)}, f32[4,1024]{1,0:T(4,128)S(1)}, f32[4,1024,128]{2,1,0:T(8,128)})) conditional(s32[]{:T(128)} %convert_element_type.57, (f32[4,1024]{1,0:T(4,128)S(1)}, f32[4,1024]{1,0:T(4,128)S(1)}, f32[4,1024,128]{2,1,0:T(8,128)}) %tuple.90, (pred[1024,512]{0,1:T(8,128)(4,1)S(1)}, bf16[32768,128]{1,0:T(8,128)(2,1)}, ...), branch_computations={%region_2.2_spmd, %region_3.0_spmd} | conditional | flops 1102061568 | bytes 49284184 | solution.py:63
  487.3 10.3 %conditional.4 = ((f32[4,1024]{1,0:T(4,128)S(1)}, f32[4,1024]{1,0:T(4,128)S(1)}, f32[4,1024,128]{2,1,0:T(8,128)})) conditional(s32[]{:T(128)} %convert_element_type.57, (f32[4,1024]{1,0:T(4,128)S(1)}, f32[4,1024]{1,0:T(4,128)S(1)}, f32[4,1024,128]{2,1,0:T(8,128)}) %tuple.90, (pred[1024,512]{0,1:T(8,128)(4,1)S(1)}, bf16[32768,128]{1,0:T(8,128)(2,1)}, ...), branch_computations={%region_2.2_spmd, %region_3.0_spmd} | conditional | flops 1102061568 | bytes 49284184 | solution.py:63
  504.1 10.3 %conditional.4 = ((f32[4,1024]{1,0:T(4,128)S(1)}, f32[4,1024]{1,0:T(4,128)S(1)}, f32[4,1024,128]{2,1,0:T(8,128)})) conditional(s32[]{:T(128)} %convert_element_type.57, (f32[4,1024]{1,0:T(4,128)S(1)}, f32[4,1024]{1,0:T(4,128)S(1)}, f32[4,1024,128]{2,1,0:T(8,128)}) %tuple.90, (pred[1024,512]{0,1:T(8,128)(4,1)S(1)}, bf16[32768,128]{1,0:T(8,128)(2,1)}, ...), branch_computations={%region_2.2_spmd, %region_3.0_spmd} | conditional | flops 1102061568 | bytes 49284184 | solution.py:63
  516.6 10.3 %conditional.4 = ((f32[4,1024]{1,0:T(4,128)S(1)}, f32[4,1024]{1,0:T(4,128)S(1)}, f32[4,1024,128]{2,1,0:T(8,128)})) conditional(s32[]{:T(128)} %convert_element_type.57, (f32[4,1024]{1,0:T(4,128)S(1)}, f32[4,1024]{1,0:T(4,128)S(1)}, f32[4,1024,128]{2,1,0:T(8,128)}) %tuple.90, (pred[1024,512]{0,1:T(8,128)(4,1)S(1)}, bf16[32768,128]{1,0:T(8,128)(2,1)}, ...), branch_computations={%region_2.2_spmd, %region_3.0_spmd} | conditional | flops 1102061568 | bytes 49284184 | solution.py:63
  533.4 10.3 %conditional.4 = ((f32[4,1024]{1,0:T(4,128)S(1)}, f32[4,1024]{1,0:T(4,128)S(1)}, f32[4,1024,128]{2,1,0:T(8,128)})) conditional(s32[]{:T(128)} %convert_element_type.57, (f32[4,1024]{1,0:T(4,128)S(1)}, f32[4,1024]{1,0:T(4,128)S(1)}, f32[4,1024,128]{2,1,0:T(8,128)}) %tuple.90, (pred[1024,512]{0,1:T(8,128)(4,1)S(1)}, bf16[32768,128]{1,0:T(8,128)(2,1)}, ...), branch_computations={%region_2.2_spmd, %region_3.0_spmd} | conditional | flops 1102061568 | bytes 49284184 | solution.py:63
  545.9 10.3 %conditional.4 = ((f32[4,1024]{1,0:T(4,128)S(1)}, f32[4,1024]{1,0:T(4,128)S(1)}, f32[4,1024,128]{2,1,0:T(8,128)})) conditional(s32[]{:T(128)} %convert_element_type.57, (f32[4,1024]{1,0:T(4,128)S(1)}, f32[4,1024]{1,0:T(4,128)S(1)}, f32[4,1024,128]{2,1,0:T(8,128)}) %tuple.90, (pred[1024,512]{0,1:T(8,128)(4,1)S(1)}, bf16[32768,128]{1,0:T(8,128)(2,1)}, ...), branch_computations={%region_2.2_spmd, %region_3.0_spmd} | conditional | flops 1102061568 | bytes 49284184 | solution.py:63
  560.5 10.3 %conditional.4 = ((f32[4,1024]{1,0:T(4,128)S(1)}, f32[4,1024]{1,0:T(4,128)S(1)}, f32[4,1024,128]{2,1,0:T(8,128)})) conditional(s32[]{:T(128)} %convert_element_type.57, (f32[4,1024]{1,0:T(4,128)S(1)}, f32[4,1024]{1,0:T(4,128)S(1)}, f32[4,1024,128]{2,1,0:T(8,128)}) %tuple.90, (pred[1024,512]{0,1:T(8,128)(4,1)S(1)}, bf16[32768,128]{1,0:T(8,128)(2,1)}, ...), branch_computations={%region_2.2_spmd, %region_3.0_spmd} | conditional | flops 1102061568 | bytes 49284184 | solution.py:63
  573.0 10.3 %conditional.4 = ((f32[4,1024]{1,0:T(4,128)S(1)}, f32[4,1024]{1,0:T(4,128)S(1)}, f32[4,1024,128]{2,1,0:T(8,128)})) conditional(s32[]{:T(128)} %convert_element_type.57, (f32[4,1024]{1,0:T(4,128)S(1)}, f32[4,1024]{1,0:T(4,128)S(1)}, f32[4,1024,128]{2,1,0:T(8,128)}) %tuple.90, (pred[1024,512]{0,1:T(8,128)(4,1)S(1)}, bf16[32768,128]{1,0:T(8,128)(2,1)}, ...), branch_computations={%region_2.2_spmd, %region_3.0_spmd} | conditional | flops 1102061568 | bytes 49284184 | solution.py:63
  585.5 10.3 %conditional.4 = ((f32[4,1024]{1,0:T(4,128)S(1)}, f32[4,1024]{1,0:T(4,128)S(1)}, f32[4,1024,128]{2,1,0:T(8,128)})) conditional(s32[]{:T(128)} %convert_element_type.57, (f32[4,1024]{1,0:T(4,128)S(1)}, f32[4,1024]{1,0:T(4,128)S(1)}, f32[4,1024,128]{2,1,0:T(8,128)}) %tuple.90, (pred[1024,512]{0,1:T(8,128)(4,1)S(1)}, bf16[32768,128]{1,0:T(8,128)(2,1)}, ...), branch_computations={%region_2.2_spmd, %region_3.0_spmd} | conditional | flops 1102061568 | bytes 49284184 | solution.py:63
  597.9 10.3 %conditional.4 = ((f32[4,1024]{1,0:T(4,128)S(1)}, f32[4,1024]{1,0:T(4,128)S(1)}, f32[4,1024,128]{2,1,0:T(8,128)})) conditional(s32[]{:T(128)} %convert_element_type.57, (f32[4,1024]{1,0:T(4,128)S(1)}, f32[4,1024]{1,0:T(4,128)S(1)}, f32[4,1024,128]{2,1,0:T(8,128)}) %tuple.90, (pred[1024,512]{0,1:T(8,128)(4,1)S(1)}, bf16[32768,128]{1,0:T(8,128)(2,1)}, ...), branch_computations={%region_2.2_spmd, %region_3.0_spmd} | conditional | flops 1102061568 | bytes 49284184 | solution.py:63
  610.4 10.3 %conditional.4 = ((f32[4,1024]{1,0:T(4,128)S(1)}, f32[4,1024]{1,0:T(4,128)S(1)}, f32[4,1024,128]{2,1,0:T(8,128)})) conditional(s32[]{:T(128)} %convert_element_type.57, (f32[4,1024]{1,0:T(4,128)S(1)}, f32[4,1024]{1,0:T(4,128)S(1)}, f32[4,1024,128]{2,1,0:T(8,128)}) %tuple.90, (pred[1024,512]{0,1:T(8,128)(4,1)S(1)}, bf16[32768,128]{1,0:T(8,128)(2,1)}, ...), branch_computations={%region_2.2_spmd, %region_3.0_spmd} | conditional | flops 1102061568 | bytes 49284184 | solution.py:63
  625.1 10.3 %conditional.4 = ((f32[4,1024]{1,0:T(4,128)S(1)}, f32[4,1024]{1,0:T(4,128)S(1)}, f32[4,1024,128]{2,1,0:T(8,128)})) conditional(s32[]{:T(128)} %convert_element_type.57, (f32[4,1024]{1,0:T(4,128)S(1)}, f32[4,1024]{1,0:T(4,128)S(1)}, f32[4,1024,128]{2,1,0:T(8,128)}) %tuple.90, (pred[1024,512]{0,1:T(8,128)(4,1)S(1)}, bf16[32768,128]{1,0:T(8,128)(2,1)}, ...), branch_computations={%region_2.2_spmd, %region_3.0_spmd} | conditional | flops 1102061568 | bytes 49284184 | solution.py:63
  637.5 10.3 %conditional.4 = ((f32[4,1024]{1,0:T(4,128)S(1)}, f32[4,1024]{1,0:T(4,128)S(1)}, f32[4,1024,128]{2,1,0:T(8,128)})) conditional(s32[]{:T(128)} %convert_element_type.57, (f32[4,1024]{1,0:T(4,128)S(1)}, f32[4,1024]{1,0:T(4,128)S(1)}, f32[4,1024,128]{2,1,0:T(8,128)}) %tuple.90, (pred[1024,512]{0,1:T(8,128)(4,1)S(1)}, bf16[32768,128]{1,0:T(8,128)(2,1)}, ...), branch_computations={%region_2.2_spmd, %region_3.0_spmd} | conditional | flops 1102061568 | bytes 49284184 | solution.py:63
  650.0 10.3 %conditional.4 = ((f32[4,1024]{1,0:T(4,128)S(1)}, f32[4,1024]{1,0:T(4,128)S(1)}, f32[4,1024,128]{2,1,0:T(8,128)})) conditional(s32[]{:T(128)} %convert_element_type.57, (f32[4,1024]{1,0:T(4,128)S(1)}, f32[4,1024]{1,0:T(4,128)S(1)}, f32[4,1024,128]{2,1,0:T(8,128)}) %tuple.90, (pred[1024,512]{0,1:T(8,128)(4,1)S(1)}, bf16[32768,128]{1,0:T(8,128)(2,1)}, ...), branch_computations={%region_2.2_spmd, %region_3.0_spmd} | conditional | flops 1102061568 | bytes 49284184 | solution.py:63
  662.4 10.3 %conditional.4 = ((f32[4,1024]{1,0:T(4,128)S(1)}, f32[4,1024]{1,0:T(4,128)S(1)}, f32[4,1024,128]{2,1,0:T(8,128)})) conditional(s32[]{:T(128)} %convert_element_type.57, (f32[4,1024]{1,0:T(4,128)S(1)}, f32[4,1024]{1,0:T(4,128)S(1)}, f32[4,1024,128]{2,1,0:T(8,128)}) %tuple.90, (pred[1024,512]{0,1:T(8,128)(4,1)S(1)}, bf16[32768,128]{1,0:T(8,128)(2,1)}, ...), branch_computations={%region_2.2_spmd, %region_3.0_spmd} | conditional | flops 1102061568 | bytes 49284184 | solution.py:63
  677.1 10.3 %conditional.4 = ((f32[4,1024]{1,0:T(4,128)S(1)}, f32[4,1024]{1,0:T(4,128)S(1)}, f32[4,1024,128]{2,1,0:T(8,128)})) conditional(s32[]{:T(128)} %convert_element_type.57, (f32[4,1024]{1,0:T(4,128)S(1)}, f32[4,1024]{1,0:T(4,128)S(1)}, f32[4,1024,128]{2,1,0:T(8,128)}) %tuple.90, (pred[1024,512]{0,1:T(8,128)(4,1)S(1)}, bf16[32768,128]{1,0:T(8,128)(2,1)}, ...), branch_computations={%region_2.2_spmd, %region_3.0_spmd} | conditional | flops 1102061568 | bytes 49284184 | solution.py:63
  691.8 10.3 %conditional.4 = ((f32[4,1024]{1,0:T(4,128)S(1)}, f32[4,1024]{1,0:T(4,128)S(1)}, f32[4,1024,128]{2,1,0:T(8,128)})) conditional(s32[]{:T(128)} %convert_element_type.57, (f32[4,1024]{1,0:T(4,128)S(1)}, f32[4,1024]{1,0:T(4,128)S(1)}, f32[4,1024,128]{2,1,0:T(8,128)}) %tuple.90, (pred[1024,512]{0,1:T(8,128)(4,1)S(1)}, bf16[32768,128]{1,0:T(8,128)(2,1)}, ...), branch_computations={%region_2.2_spmd, %region_3.0_spmd} | conditional | flops 1102061568 | bytes 49284184 | solution.py:63
  704.2 10.3 %conditional.4 = ((f32[4,1024]{1,0:T(4,128)S(1)}, f32[4,1024]{1,0:T(4,128)S(1)}, f32[4,1024,128]{2,1,0:T(8,128)})) conditional(s32[]{:T(128)} %convert_element_type.57, (f32[4,1024]{1,0:T(4,128)S(1)}, f32[4,1024]{1,0:T(4,128)S(1)}, f32[4,1024,128]{2,1,0:T(8,128)}) %tuple.90, (pred[1024,512]{0,1:T(8,128)(4,1)S(1)}, bf16[32768,128]{1,0:T(8,128)(2,1)}, ...), branch_computations={%region_2.2_spmd, %region_3.0_spmd} | conditional | flops 1102061568 | bytes 49284184 | solution.py:63
  714.6 66.9 %while.35 = (s32[]{:T(128)}, f32[4,1024]{1,0:T(4,128)S(1)}, f32[4,1024]{1,0:T(4,128)S(1)}, f32[4,1024,128]{2,1,0:T(8,128)}, s32[4096]{0:T(1024)S(1)}, /*index=5*...) while((s32[]{:T(128)}, f32[4,1024]{1,0:T(4,128)S(1)}, ...), condition=%wide.region_15.16_spmd, body=%wide.region_9.15_spmd.sunk | while | flops 1103110144 | bytes 49818980 | solution.py:79
  792.7 231.4 %reduce-scatter.2.cloned.1.call-done = bf16[1024,1024]{1,0:T(8,128)(2,1)} async-done(((bf16[1024,4096]{1,0:T(8,128)(2,1)}), bf16[1024,1024]{1,0:T(8,128)(2,1)}) %reduce-scatter.2.cloned.1.call-update) | async-done | bytes 2097168 | tf_op jit(solution)/shard_map/reduce_scatter | solution.py:114
  (759 shorter events, 688.6 us)
Async XLA Ops:
  6.5 59.5 %all-gather.5.cloned.1.call-start = ((), (), s32[]{:S(2)}) async-start(), calls=%async_computation.1 | async-start | bytes 8650752 | tf_op jit(solution)/shard_map/all_gather | solution.py:96
  7.3 113.5 %all-gather.7.cloned.1.call-start = ((), (), s32[]{:S(2)}) async-start(), calls=%async_computation.2 | async-start | bytes 8650752 | tf_op jit(solution)/shard_map/all_gather | solution.py:97
  8.0 706.5 %all-gather.11.cloned.1.call-start = ((), (), s32[]{:S(2)}) async-start(), calls=%async_computation.4 | async-start | bytes 1081344 | tf_op jit(solution)/shard_map/all_gather | solution.py:102
  8.7 705.8 %all-gather.9.cloned.1.call-start = ((), (), s32[]{:S(2)}) async-start(), calls=%async_computation.3 | async-start | bytes 1081344 | tf_op jit(solution)/shard_map/all_gather | solution.py:101
  9.3 1014.7 %reduce-scatter.2.cloned.1.call-start = ((), (), s32[]{:S(2)}) async-start(), calls=%async_computation.5 | async-start | bytes 10485760 | tf_op jit(solution)/shard_map/reduce_scatter | solution.py:114
  128.8 4.9 copy-start.1
  141.2 4.9 copy-start.1
  153.7 4.9 copy-start.1
  166.2 4.9 copy-start.1
  178.6 4.9 copy-start.1
  191.1 4.9 copy-start.1
  205.8 4.9 copy-start.1
  218.2 4.9 copy-start.1
  245.4 4.9 copy-start.1
  260.0 4.9 copy-start.1
  272.5 4.9 copy-start.1
  285.0 4.9 copy-start.1
  297.4 4.9 copy-start.1
  309.9 4.9 copy-start.1
  324.5 4.9 copy-start.1
  337.0 4.9 copy-start.1
  349.5 4.9 copy-start.1
  361.9 4.9 copy-start.1
  374.4 4.9 copy-start.1
  386.9 4.9 copy-start.1
  403.7 4.9 copy-start.1
  416.2 4.9 copy-start.1
  433.0 4.9 copy-start.1
  447.7 4.9 copy-start.1
  460.1 4.9 copy-start.1
  474.8 4.9 copy-start.1
  487.3 4.9 copy-start.1
  504.1 4.9 copy-start.1
  516.6 4.9 copy-start.1
  560.6 4.9 copy-start.1
  573.0 4.9 copy-start.1
  625.1 4.9 copy-start.1
  637.5 4.9 copy-start.1
  650.0 4.9 copy-start.1
  662.5 4.9 copy-start.1
  677.1 4.9 copy-start.1
  691.8 4.9 copy-start.1
  704.2 4.9 copy-start.1
  718.6 4.9 copy-start.3
  730.8 4.9 copy-start.3
  746.8 4.9 copy-start.3
  759.0 4.9 copy-start.3
  771.2 4.9 copy-start.3
  (56 other events, 97.5 us)
Sparse Core Ops, SparseCore 0:
  9.6 56.3 all-gather.4
  68.3 52.3 all-gather.6
  123.0 42.2 all-gather.10
  167.5 42.0 all-gather.8
  792.8 231.2 reduce-scatter.1
where the time goes:
time: 1030 us
  waiting for transfers between devices  341 us (33%)
  matrix products  341 us (33%)
  other arithmetic  200 us (19%)
  local copies, waits for them, and re-layouts  82.1 us (8%)
  loops' own time  53 us (5%)
  between operations  13.2 us (1%)
    reduce_scatter x1, waiting for transfers between devices, on_device(): lax.psum_scatter(partial_term.astype(jnp.bfloat16), 'head', scatter_dimen...  231 us
    dot_general x49, matrix products, update(): jnp.einsum('hqk,kd->hqd', weight.astype(jnp.bfloat16), value_block, prefe...  201 us
    dot_general x49, matrix products, update(): jnp.einsum('qhd,kd->hqk', query_three, key_block, preferred_element_type=...  131 us
    reduce_sum x49, other arithmetic, update(): new_total = running_total * factor + jnp.sum(weight, axis=-1)  103 us
    reduce_or x64, other arithmetic, attend(): jnp.any(key_mask)  84.1 us
    cond x245, local copies, waits for them, and re-layouts  64.8 us
    all_gather x1, waiting for transfers between devices, on_device(): lax.all_gather(row_values, 'ctx', axis=0, tiled=True)  54.7 us
    all_gather x1, waiting for transfers between devices, on_device(): lax.all_gather(row_keys, 'ctx', axis=0, tiled=True)  51.8 us
  transfers between devices with their start and end apart: 5, of which 3 were waited for; matrix products, arithmetic and copies ran while one was open for 48% of the time, Pallas kernels for 0%

commit v1 on v0

v1 whole, which is shorter than its diff:
```python
import functools

import jax
import jax.numpy as jnp
from jax import lax
from jax.experimental import pallas as pl
from jax.experimental.pallas import tpu as pltpu
from jax.sharding import PartitionSpec as P

BLK = 128
UNSEEN = -2e30
LOWEST = -1e30
FAR = 1 << 24


def attend_kernel(
    scale, heads, order_ref, count_ref, base_ref, bounds_ref, q_ref, kv_ref, out_ref, qt_ref, acc_ref, top_ref
):
    blocks = q_ref.shape[0] // BLK
    size = q_ref.shape[1] // heads
    wide = heads * BLK
    half = wide // 2
    row_span = base_ref.shape[0] // 9 * 8 * BLK
    ones = jnp.ones((16, 2 * BLK), jnp.bfloat16)
    key_row = lax.broadcasted_iota(jnp.int32, (BLK, half), 0)

    def one_block(j, _):
        rows = pl.ds(pl.multiple_of(j * BLK, BLK), BLK)
        for h in range(heads):
            qt_ref[:, h * BLK : (h + 1) * BLK] = q_ref[rows, h * size : (h + 1) * size].T
        top_ref[...] = jnp.full(top_ref.shape, LOWEST, jnp.float32)
        acc_ref[...] = jnp.zeros(acc_ref.shape, jnp.float32)
        full = count_ref[j, 0] // 2
        seen = count_ref[j, 1]

        def tile(t, masked):
            first, second = order_ref[j, 2 * t], order_ref[j, 2 * t + 1]
            one, two = kv_ref[first], kv_ref[second]
            keys = jnp.concatenate([one[:, :size], two[:, :size]], axis=0)
            values = jnp.concatenate([one[:, size:], two[:, size:]], axis=1)
            values = jnp.concatenate([values, ones], axis=0)
            for part in range(2):
                cols = slice(part * half, (part + 1) * half)
                score = jnp.dot(keys, qt_ref[:, cols], preferred_element_type=jnp.float32)
                if masked:
                    pieces = []
                    for n, index in enumerate((first, second)):
                        base = jnp.where(2 * t + n < seen, base_ref[index], FAR)
                        cached = base >= row_span
                        low = jnp.where(cached, bounds_ref[j, 2:3, cols], bounds_ref[j, 0:1, cols])
                        high = jnp.where(cached, bounds_ref[j, 3:4, cols], bounds_ref[j, 1:2, cols])
                        row = key_row + base
                        piece = score[n * BLK : (n + 1) * BLK]
                        pieces.append(jnp.where((row >= low) & (row <= high), piece, UNSEEN))
                    score = jnp.concatenate(pieces, axis=0)
                old = top_ref[0:1, cols]
                new = jnp.maximum(old, jnp.max(score, axis=0, keepdims=True))
                weight = jnp.exp2(score * scale - new * scale).astype(jnp.bfloat16)
                factor = jnp.exp2((old - new) * scale)
                top_ref[0:1, cols] = new
                acc_ref[:, cols] = acc_ref[:, cols] * factor + jnp.dot(
                    values, weight, preferred_element_type=jnp.float32
                )

        def plain(t, _):
            tile(t, False)
            return 0

        def edge(t, _):
            tile(t, True)
            return 0

        lax.fori_loop(0, full, plain, 0)
        lax.fori_loop(full, (seen + 1) // 2, edge, 0)
        for h in range(heads):
            cols = slice(h * BLK, (h + 1) * BLK)
            result = acc_ref[:size, cols] / acc_ref[size : size + 1, cols]
            out_ref[rows, h * size : (h + 1) * size] = result.T.astype(out_ref.dtype)
        return 0

    lax.fori_loop(0, blocks, one_block, 0)


def attend(queries, kv, order, count, base, bounds, heads, size):
    wide = heads * BLK
    scale = 1.4426950408889634 / size**0.5
    smem = pl.BlockSpec(memory_space=pltpu.SMEM)
    vmem = pl.BlockSpec(memory_space=pltpu.VMEM)
    return pl.pallas_call(
        functools.partial(attend_kernel, scale, heads),
        out_shape=jax.ShapeDtypeStruct(queries.shape, jnp.bfloat16),
        in_specs=[smem, smem, smem, vmem, vmem, vmem],
        out_specs=vmem,
        scratch_shapes=[
            pltpu.VMEM((size, wide), jnp.bfloat16),
            pltpu.VMEM((size + 16, wide), jnp.float32),
            pltpu.VMEM((8, wide), jnp.float32),
        ],
        compiler_params=pltpu.CompilerParams(vmem_limit_bytes=48 << 20),
        cost_estimate=pl.CostEstimate(flops=8 << 30, bytes_accessed=24 << 20, transcendentals=8 << 20),
        name="attend",
    )(order, count, base, bounds, queries, kv)


def plan(doc_ids, prefix_lens, block_order, shard_index, local_blocks, shards, heads):
    block_count = block_order.shape[0]
    rows = doc_ids.shape[0]
    inside = jnp.arange(BLK, dtype=jnp.int32)
    mine = lax.dynamic_slice_in_dim(block_order, shard_index * local_blocks, local_blocks, 0)
    doc = doc_ids.reshape(block_count, BLK)[mine]
    position = mine[:, None] * BLK + inside[None, :]
    docs = jnp.arange(prefix_lens.shape[0], dtype=jnp.int32)
    doc_start = jnp.sum((doc_ids[None, :] < docs[:, None]).astype(jnp.int32), axis=1)
    prefix_end = jnp.cumsum(prefix_lens)
    prefix_start = prefix_end - prefix_lens
    chosen = doc[:, :, None] == docs[None, None, :]
    pick = lambda table: jnp.sum(jnp.where(chosen, table[None, None, :], 0), axis=2)
    low_row, high_row = pick(doc_start), position
    low_cached, high_cached = pick(prefix_start) + rows, pick(prefix_end) + (rows - 1)
    bounds = jnp.stack([low_row, high_row, low_cached, high_cached], axis=1)
    bounds = jnp.tile(bounds, (1, 2, heads)).astype(jnp.int32)
    row_base = block_order.reshape(shards, local_blocks) * BLK
    cached_base = rows + jnp.arange(shards, dtype=jnp.int32)[:, None] * BLK
    base = jnp.concatenate([row_base, cached_base], axis=1).reshape(-1)
    index = jnp.arange(base.shape[0], dtype=jnp.int32)
    cached = (base >= rows)[None, :]
    ends = lambda array, at: array[:, at][:, None]
    first = base[None, :]
    last = first + (BLK - 1)
    seen = jnp.where(
        cached,
        (last >= ends(low_cached, 0)) & (first <= ends(high_cached, -1)),
        (last >= ends(low_row, 0)) & (first <= ends(high_row, -1)),
    )
    whole = jnp.where(
        cached,
        (first >= ends(low_cached, -1)) & (last <= ends(high_cached, 0)),
        (first >= ends(low_row, -1)) & (last <= ends(high_row, 0)),
    )
    key = jnp.where(whole, index[None, :], jnp.where(seen, 1024 + index[None, :], 4096 + index[None, :]))
    order = jnp.sort(key, axis=1) % 1024
    count = jnp.stack([jnp.sum(whole, axis=1), jnp.sum(seen, axis=1)], axis=1).astype(jnp.int32)
    return order, count, base, bounds


def on_device(
    queries,
    row_keys,
    row_values,
    cached_keys,
    cached_values,
    doc_ids,
    prefix_lens,
    block_order,
    out_weight,
):
    size = row_keys.shape[1]
    heads = queries.shape[1] // size
    local_blocks = queries.shape[0] // BLK
    shards = lax.axis_size("ctx")
    keys = jnp.concatenate([row_keys, cached_keys], axis=0).reshape(-1, BLK, size)
    values = jnp.concatenate([row_values, cached_values], axis=0).reshape(-1, BLK, size)
    packed = jnp.concatenate([keys, jnp.swapaxes(values, 1, 2)], axis=2)
    gathered = lax.all_gather(packed, "ctx", axis=0, tiled=True)
    weight = lax.all_to_all(out_weight, "head", 1, 0, tiled=True)
    order, count, base, bounds = plan(
        doc_ids, prefix_lens, block_order, lax.axis_index("ctx"), local_blocks, shards, heads
    )
    gathered, weight = lax.optimization_barrier((gathered, weight))
    attended = attend(queries, gathered, order, count, base, bounds, heads, size)
    attended = lax.all_gather(attended, "head", axis=1, tiled=True)
    return jnp.dot(attended, weight, preferred_element_type=jnp.float32).astype(jnp.bfloat16)


def solution(mesh):
    placed = (
        P("ctx", "head"),
        P("ctx", None),
        P("ctx", None),
        P("ctx", None),
        P("ctx", None),
        P(),
        P(),
        P(),
        P("head", None),
    )
    return jax.shard_map(
        on_device, mesh=mesh, in_specs=placed, out_specs=P("ctx", "head"), check_vma=False
    )
```

time: 1030 us -> 219 us (0.21)
  matrix products: 341 us -> 9.27 us
  waiting for transfers between devices: 341 us -> 134 us
  other arithmetic: 200 us -> 8.14 us
  local copies, waits for them, and re-layouts: 82.1 us -> 14.8 us
  loops' own time: 53 us -> 0 us
  Pallas kernels: 0 us -> 36 us
    dot_general x99 -> x1, matrix products: 341 us -> 9.27 us  [on_device(): jnp.dot(attended, weight, preferred_element_type=jnp.float32)]
    reduce_scatter x1 -> x0, waiting for transfers between devices: 231 us -> none  [on_device(): lax.psum_scatter(partial_term.astype(jnp.bfloat16), 'head', scatter_dimen...]
    reduce_sum x50 -> x3, other arithmetic: 104 us -> 0.83 us  [the longest x1 0.51 us: plan(): jnp.sum((doc_ids[None, :] < docs[:, None]).astype(jnp.int32), axis=1)]
    reduce_or x64 -> x0, other arithmetic: 84.1 us -> none  [attend(): jnp.any(key_mask)]
    cond x245 -> x0, local copies, waits for them, and re-layouts: 64.8 us -> none
    another operation x74 -> x0, loops' own time: 53 us -> none  [the longest x2 49.1 us: sweep(): return lax.fori_loop(0, count // width, one_step, carry)]
    all_to_all x0 -> x1, waiting for transfers between devices: none -> 42 us  [on_device(): weight = lax.all_to_all(out_weight, 'head', 1, 0, tiled=True)]
    pallas_call x0 -> x1, Pallas kernels: none -> 36 us  [attend(): pl.pallas_call(functools.partial(attend_kernel, scale, heads), out_shape=...]
  transfers between devices with their start and end apart: 5 -> 3, of which waited for: 3 -> 3; matrix products, arithmetic and copies ran while one was open for 48% -> 9% of each run, Pallas kernels for 0% -> 0%
where the time goes in v1:
time: 219 us; the launch traced here: 222 us
  waiting for transfers between devices  134 us (61%)
  Pallas kernels  36 us (16%)
  local copies, waits for them, and re-layouts  14.8 us (7%)
  between operations  13.5 us (6%)
  matrix products  9.27 us (4%)
  other arithmetic  8.14 us (4%)
  starting transfers between devices  6 us (3%)
    all_gather x1, waiting for transfers between devices, on_device(): attended = lax.all_gather(attended, 'head', axis=1, tiled=True)  77.7 us
    all_to_all x1, waiting for transfers between devices, on_device(): weight = lax.all_to_all(out_weight, 'head', 1, 0, tiled=True)  42 us
    pallas_call x1, Pallas kernels, attend(): pl.pallas_call(functools.partial(attend_kernel, scale, heads), out_shape=...  36 us
    all_gather x1, waiting for transfers between devices, on_device(): gathered = lax.all_gather(packed, 'ctx', axis=0, tiled=True)  14.1 us
    dot_general x1, matrix products, on_device(): jnp.dot(attended, weight, preferred_element_type=jnp.float32)  9.27 us
    all_to_all x1, local copies, waits for them, and re-layouts, on_device(): weight = lax.all_to_all(out_weight, 'head', 1, 0, tiled=True)  6.58 us
    unnamed x9, local copies, waits for them, and re-layouts  6.5 us
    all_to_all x1, starting transfers between devices, on_device(): weight = lax.all_to_all(out_weight, 'head', 1, 0, tiled=True)  5.99 us
  transfers between devices with their start and end apart: 3, of which 3 were waited for; matrix products, arithmetic and copies ran while one was open for 9% of the time, Pallas kernels for 0%

profile of v1, /device:TPU:1, one launch (start us, length us, event | category | flops | bytes accessed | tf_op | source)
XLA Modules:
  0.0 221.6 jit_solution(13178199231774612849)
XLA Ops:
  6.5 0.0 all-gather.3.cloned.1.call-start
  6.5 1.0 pad_maximum_fusion.2
  7.5 0.2 copy.40
  7.7 1.0 pad_maximum_fusion.1
  8.8 0.9 pad_maximum_fusion
  9.6 0.0 all-gather.3.cloned.1.call-update
  9.7 6.5 %copy.41 = bf16[512,4096]{0,1:T(8,128)(2,1)} copy(bf16[512,4096]{1,0:T(8,128)(2,1)} %param.17) | data formatting | bytes 8388608 | tf_op args[8]
  16.2 0.0 copy-start.2
  16.2 0.0 copy-start.3
  16.2 0.0 copy-start.1
  16.2 6.0 %all-to-all-start = ((bf16[512,4,1024]{0,2,1:T(8,128)(2,1)}), bf16[512,4,1024]{0,2,1:T(8,128)(2,1)}, u32[]{:S(2)}, u32[]{:S(2)}) async-start(bf16[512,4,1024]{0,2,1:T(8,128)(2,1)} %bitcast.21), calls=%async_computation | async-start | bytes 8388608 | tf_op jit(solution)/shard_map/all_to_all | solution.py:165
  22.2 0.0 all-gather.5.cloned.1.call-start
  22.2 0.0 copy-done.2
  22.2 0.1 mul.32
  22.3 0.1 pad_add_fusion
  22.3 0.1 compare_select_fusion
  22.4 0.0 copy-done.3
  22.4 0.1 copy.38
  22.5 0.1 reduce-window.8
  22.6 0.1 reduce
  22.7 0.1 reshape.129.base_ref
  22.8 0.0 copy-done.1
  22.8 0.6 gather_fusion
  23.4 0.5 convert_reduce_fusion
  23.9 0.1 select_reduce_fusion.2
  24.0 0.2 slice_reduce_fusion.2
  24.2 0.2 slice_reduce_fusion.1
  24.4 0.2 slice_reduce_fusion
  24.6 0.2 convert_reduce_fusion.1
  24.9 0.1 copy.43.count_ref
  24.9 0.1 iota_add_fusion.1
  25.0 0.1 tile.10.bounds_ref
  25.1 3.9 %sort.15 = (s32[8,288]{1,0:T(8,128)S(1)}, s32[8,288]{1,0:T(8,128)}) sort(s32[8,288]{1,0:T(8,128)S(1)} %select_select_fusion, s32[8,288]{1,0:T(8,128)S(1)} %iota.33), dimensions={1}, to_apply=%region_5.6 | sort | flops 27648 | bytes 36864 | tf_op jit(solution)/shard_map/jit(sort)/sort | solution.py:141
  29.1 42.0 %all-to-all-done = bf16[512,4,1024]{0,2,1:T(8,128)(2,1)} async-done(((bf16[512,4,1024]{0,2,1:T(8,128)(2,1)}), bf16[512,4,1024]{0,2,1:T(8,128)(2,1)}, u32[]{:S(2)}, u32[]{:S(2)}) %all-to-all-start) | async-done | bytes 4194336 | tf_op jit(solution)/shard_map/all_to_all | solution.py:165
  71.1 0.0 copy-start
  71.1 6.6 %copy.42 = bf16[4,512,1024]{2,1,0:T(8,128)(2,1)} copy(bf16[4,512,1024]{1,2,0:T(8,128)(2,1)} %bitcast.13) | data formatting | bytes 8388608 | tf_op jit(solution)/shard_map/all_to_all | solution.py:165
  77.7 14.1 %all-gather.3.cloned.1.call-done.kv_ref = bf16[288,128,256]{2,1,0:T(8,128)(2,1)} async-done(((bf16[9,128,256]{2,1,0:T(8,128)(2,1)}), bf16[288,128,256]{2,1,0:T(8,128)(2,1)}) %all-gather.3.cloned.1.call-update) | async-done | bytes 18874384 | tf_op jit(solution)/shard_map/all_gather | solution.py:164
  91.8 0.0 copy-done
  91.8 36.0 %attend.1 = bf16[1024,512]{1,0:T(8,128)(2,1)} custom-call(s32[8,288]{1,0:T(8,128)S(1)} %add_select_fusion.order_ref, s32[8,2]{1,0:T(8,128)S(1)} %copy.43.count_ref, s32[288]{0:T(512)S(1)} %reshape.129.base_ref, s32[8,8,512]{2,1,0:T(8,128)S(1)} %tile.10.bounds_ref, bf16[1024,512]{1,0:T(8,128)(2,1)S(1)} %copy-done, ...), custom_call_target="tpu_custom_call" | custom-call | flops 8589934592 | bytes 25165824 | tf_op jit(solution)/shard_map/attend/pallas_call | solution.py:89
  127.8 0.0 all-gather.5.cloned.1.call-update
  127.8 77.7 %all-gather.5.cloned.1.call-done = bf16[1024,2048]{1,0:T(8,128)(2,1)} async-done(((bf16[1024,512]{1,0:T(8,128)(2,1)}), bf16[1024,2048]{1,0:T(8,128)(2,1)}) %all-gather.5.cloned.1.call-update) | async-done | bytes 4194320 | tf_op jit(solution)/shard_map/all_gather | solution.py:171
  205.5 9.3 %convolution_convert_fusion = bf16[1024,1024]{1,0:T(8,128)(2,1)} fusion(bf16[1024,2048]{1,0:T(8,128)(2,1)} %all-gather.5.cloned.1.call-done, bf16[2048,1024]{1,0:T(8,128)(2,1)} %bitcast.22), kind=kOutput, calls=%fused_computation.3 | convolution fusion | flops 4296015872 | bytes 10485760 | tf_op jit(solution)/shard_map/dot_general | solution.py:172
  (17 shorter events, 0.1 us)
Async XLA Ops:
  6.5 85.3 %all-gather.3.cloned.1.call-start = ((), (), s32[]{:S(2)}) async-start(), calls=%async_computation.1 | async-start | bytes 19464192 | tf_op jit(solution)/shard_map/all_gather | solution.py:164
  16.2 6.0 %copy-start.2 = (s32[256]{0:T(256)S(1)}, s32[256]{0:T(256)}, u32[]{:S(2)}) copy-start(s32[256]{0:T(256)} %param.16) | copy-start | bytes 3076
  16.2 6.3 %copy-start.3 = (s32[32]{0:T(128)S(1)}, s32[32]{0:T(128)}, u32[]{:S(2)}) copy-start(s32[32]{0:T(128)} %param.15) | copy-start | bytes 388
  16.2 6.7 %copy-start.1 = (s32[32768]{0:T(1024)S(1)}, s32[32768]{0:T(1024)}, u32[]{:S(2)}) copy-start(s32[32768]{0:T(1024)} %param.14) | copy-start | bytes 393220
  16.2 54.9 %all-to-all-start = ((bf16[512,4,1024]{0,2,1:T(8,128)(2,1)}), bf16[512,4,1024]{0,2,1:T(8,128)(2,1)}, u32[]{:S(2)}, u32[]{:S(2)}) async-start(bf16[512,4,1024]{0,2,1:T(8,128)(2,1)} %bitcast.21), calls=%async_computation | async-start | bytes 8388608 | tf_op jit(solution)/shard_map/all_to_all | solution.py:165
  22.2 183.4 %all-gather.5.cloned.1.call-start = ((), (), s32[]{:S(2)}) async-start(), calls=%async_computation.2 | async-start | bytes 5242880 | tf_op jit(solution)/shard_map/all_gather | solution.py:171
  71.1 20.7 %copy-start = (bf16[1024,512]{1,0:T(8,128)(2,1)S(1)}, bf16[1024,512]{1,0:T(8,128)(2,1)}, u32[]{:S(2)}) copy-start(bf16[1024,512]{1,0:T(8,128)(2,1)} %q_ref.1) | copy-start | bytes 3145732
Sparse Core Ops, SparseCore 0:
  9.8 81.9 all-gather.2
  127.9 77.5 all-gather.4

commit v2 on v1

v2 whole, which is shorter than its diff:
```python
import functools

import jax
import jax.numpy as jnp
from jax import lax
from jax.experimental import pallas as pl
from jax.experimental.pallas import tpu as pltpu
from jax.sharding import Mesh
from jax.sharding import PartitionSpec as P

BLK = 128
TILE = 4
UNSEEN = -2e30
LOWEST = -1e30
FAR = 1 << 24
CTX = ("x", "y", "core")


def attend_kernel(scale, row_span, first_stage, last_stage, begin, blocks, pieces, *refs):
    order_ref, count_ref, base_ref, bounds_ref, qt_ref = refs[:5]
    refs = refs[5:]
    piece_refs, refs = refs[:pieces], refs[pieces:]
    if not first_stage:
        acc_in, top_in, *refs = refs
    if last_stage:
        out_ref, *refs = refs
    else:
        acc_out, top_out, *refs = refs
    kv_ref, acc_ref, top_ref, score_a, score_b, tile_row, tile_first, tile_kind, sems = refs
    size = qt_ref.shape[1]
    wide = qt_ref.shape[2]
    half = wide // 2
    heads = wide // BLK
    depth = TILE * BLK
    span = acc_ref.shape[1]

    copies = []
    at = 0
    for n, piece in enumerate(piece_refs):
        count = piece.shape[0]
        copies.append(pltpu.make_async_copy(piece, kv_ref.at[pl.ds(at, count)], sems.at[n]))
        at += count
    if not first_stage:
        copies.append(pltpu.make_async_copy(acc_in.at[pl.ds(begin, blocks)], acc_ref, sems.at[pieces]))
        copies.append(pltpu.make_async_copy(top_in.at[pl.ds(begin, blocks)], top_ref, sems.at[pieces + 1]))
    for copy in copies:
        copy.start()
    if first_stage:
        acc_ref[...] = jnp.zeros(acc_ref.shape, jnp.float32)
        top_ref[...] = jnp.full(top_ref.shape, LOWEST, jnp.float32)

    def list_row(j, t):
        whole, seen = count_ref[begin + j, 0], count_ref[begin + j, 1]

        def list_tile(i, t):
            tile_row[t] = j
            tile_first[t] = i * TILE
            tile_kind[t] = jnp.where(i * TILE + TILE <= whole, TILE + 1, jnp.minimum(seen - i * TILE, TILE))
            return t + 1

        return lax.fori_loop(0, (seen + (TILE - 1)) // TILE, list_tile, t)

    tiles = lax.fori_loop(0, blocks, list_row, 0)
    for n in range(2):
        tile_row[tiles + n] = 0
        tile_first[tiles + n] = 0
        tile_kind[tiles + n] = 0
    for copy in copies:
        copy.wait()

    ones = jnp.ones((span - size, depth), jnp.bfloat16)
    key_row = lax.broadcasted_iota(jnp.int32, (BLK, half), 0)

    def indices(t):
        j, first = tile_row[t] + begin, tile_first[t]
        return [order_ref[j, first + n] for n in range(TILE)]

    def score(t, score_ref):
        keys = jnp.concatenate([kv_ref[index, :, :size] for index in indices(t)], axis=0)
        j = tile_row[t] + begin
        for part in range(2):
            cols = slice(part * half, (part + 1) * half)
            score_ref[:, cols] = jnp.dot(keys, qt_ref[j, :, cols], preferred_element_type=jnp.float32)

    def fold(t, score_ref, masked):
        picked = indices(t)
        values = jnp.concatenate([kv_ref[index, :, size:] for index in picked], axis=1)
        values = jnp.concatenate([values, ones], axis=0)
        j = tile_row[t]
        kind = tile_kind[t]
        for part in range(2):
            cols = slice(part * half, (part + 1) * half)
            if masked:
                shown = []
                for n, index in enumerate(picked):
                    base = jnp.where(n < kind, base_ref[index], FAR)
                    cached = base >= row_span
                    low = jnp.where(cached, bounds_ref[begin + j, 2:3, cols], bounds_ref[begin + j, 0:1, cols])
                    high = jnp.where(cached, bounds_ref[begin + j, 3:4, cols], bounds_ref[begin + j, 1:2, cols])
                    row = key_row + base
                    piece = score_ref[n * BLK : (n + 1) * BLK, cols]
                    shown.append(jnp.where((row >= low) & (row <= high), piece, UNSEEN))
                scores = jnp.concatenate(shown, axis=0)
            else:
                scores = score_ref[:, cols]
            old = top_ref[j, 0:1, cols]
            new = jnp.maximum(old, jnp.max(scores, axis=0, keepdims=True))
            weight = jnp.exp2(scores * scale - new * scale).astype(jnp.bfloat16)
            factor = jnp.exp2((old - new) * scale)
            top_ref[j, 0:1, cols] = new
            acc_ref[j, :, cols] = acc_ref[j, :, cols] * factor + jnp.dot(
                values, weight, preferred_element_type=jnp.float32
            )

    def step(t, here, there):
        plain = tile_kind[t] > TILE

        @pl.when(plain)
        def _():
            score(t + 1, there)
            fold(t, here, False)

        @pl.when(jnp.logical_not(plain))
        def _():
            score(t + 1, there)
            fold(t, here, True)

    def pair(i, _):
        step(2 * i, score_a, score_b)
        step(2 * i + 1, score_b, score_a)
        return 0

    @pl.when(tiles > 0)
    def _():
        score(0, score_a)
        lax.fori_loop(0, (tiles + 1) // 2, pair, 0)

    if last_stage:

        def finish(j, _):
            rows = pl.ds(pl.multiple_of(j * BLK, BLK), BLK)
            for h in range(heads):
                cols = slice(h * BLK, (h + 1) * BLK)
                result = acc_ref[j, :size, cols] / acc_ref[j, size : size + 1, cols]
                out_ref[rows, h * size : (h + 1) * size] = result.T.astype(out_ref.dtype)
            return 0

        lax.fori_loop(0, blocks, finish, 0)
    else:
        back = [
            pltpu.make_async_copy(acc_ref, acc_out, sems.at[0]),
            pltpu.make_async_copy(top_ref, top_out, sems.at[1]),
        ]
        for copy in back:
            copy.start()
        for copy in back:
            copy.wait()


def attend(qt, pieces, stage, bounds, state, row_span, name, begin=0, blocks=None, last_stage=False):
    order, count, base = stage
    total, size, wide = qt.shape
    blocks = total if blocks is None else blocks
    first_stage = state is None
    scale = 1.4426950408889634 / size**0.5
    span = size + 16
    smem = pl.BlockSpec(memory_space=pltpu.SMEM)
    vmem = pl.BlockSpec(memory_space=pltpu.VMEM)
    hbm = pl.BlockSpec(memory_space=pl.ANY)
    held = sum(piece.shape[0] for piece in pieces)
    tiles = blocks * (held // TILE) + 2
    if last_stage:
        out_shape = jax.ShapeDtypeStruct((blocks * BLK, wide // BLK * size), jnp.bfloat16)
        out_specs = vmem
    else:
        out_shape = (
            jax.ShapeDtypeStruct((total, span, wide), jnp.float32),
            jax.ShapeDtypeStruct((total, 8, wide), jnp.float32),
        )
        out_specs = (hbm, hbm)
    return pl.pallas_call(
        functools.partial(
            attend_kernel, scale, row_span, first_stage, last_stage, begin, blocks, len(pieces)
        ),
        out_shape=out_shape,
        in_specs=[smem, smem, smem, vmem, vmem] + [hbm] * len(pieces) + [hbm] * (0 if first_stage else 2),
        out_specs=out_specs,
        scratch_shapes=[
            pltpu.VMEM((held, BLK, 2 * size), jnp.bfloat16),
            pltpu.VMEM((blocks, span, wide), jnp.float32),
            pltpu.VMEM((blocks, 8, wide), jnp.float32),
            pltpu.VMEM((TILE * BLK, wide), jnp.float32),
            pltpu.VMEM((TILE * BLK, wide), jnp.float32),
            pltpu.SMEM((tiles,), jnp.int32),
            pltpu.SMEM((tiles,), jnp.int32),
            pltpu.SMEM((tiles,), jnp.int32),
            pltpu.SemaphoreType.DMA((len(pieces) + 2,)),
        ],
        compiler_params=pltpu.CompilerParams(vmem_limit_bytes=56 << 20),
        cost_estimate=pl.CostEstimate(flops=2 << 30, bytes_accessed=8 << 20, transcendentals=2 << 20),
        name=name,
    )(order, count, base, bounds, qt, *pieces, *(() if first_stage else state))


def plan(doc_ids, prefix_lens, block_order, mine, stage_bases, heads):
    block_count = block_order.shape[0]
    rows = doc_ids.shape[0]
    inside = jnp.arange(BLK, dtype=jnp.int32)
    doc = doc_ids.reshape(block_count, BLK)[mine]
    position = mine[:, None] * BLK + inside[None, :]
    docs = jnp.arange(prefix_lens.shape[0], dtype=jnp.int32)
    doc_start = jnp.sum((doc_ids[None, :] < docs[:, None]).astype(jnp.int32), axis=1)
    prefix_end = jnp.cumsum(prefix_lens)
    prefix_start = prefix_end - prefix_lens
    chosen = doc[:, :, None] == docs[None, None, :]
    pick = lambda table: jnp.sum(jnp.where(chosen, table[None, None, :], 0), axis=2)
    low_row, high_row = pick(doc_start), position
    low_cached, high_cached = pick(prefix_start) + rows, pick(prefix_end) + (rows - 1)
    bounds = jnp.stack([low_row, high_row, low_cached, high_cached], axis=1)
    bounds = jnp.tile(bounds, (1, 2, heads)).astype(jnp.int32)
    width = max(base.shape[0] for base in stage_bases)
    fill = lambda base: jnp.pad(base, (0, width - base.shape[0]), constant_values=FAR)
    first = jnp.stack([fill(base) for base in stage_bases])[:, None, :]
    last = first + (BLK - 1)
    cached = first >= rows
    ends = lambda array, at: array[:, at][None, :, None]
    seen = jnp.where(
        cached,
        (last >= ends(low_cached, 0)) & (first <= ends(high_cached, -1)),
        (last >= ends(low_row, 0)) & (first <= ends(high_row, -1)),
    )
    whole = jnp.where(
        cached,
        (first >= ends(low_cached, -1)) & (last <= ends(high_cached, 0)),
        (first >= ends(low_row, -1)) & (last <= ends(high_row, 0)),
    )
    index = jnp.arange(width, dtype=jnp.int32)[None, None, :]
    key = jnp.where(whole, index, jnp.where(seen, 1024 + index, 4096 + index))
    order = lax.sort(key, dimension=2) % 1024
    count = jnp.stack([jnp.sum(whole, axis=2), jnp.sum(seen, axis=2)], axis=2).astype(jnp.int32)
    return [(order[n, :, : base.shape[0]], count[n], base) for n, base in enumerate(stage_bases)], bounds


def on_device(
    queries,
    row_keys,
    row_values,
    cached_keys,
    cached_values,
    doc_ids,
    prefix_lens,
    block_order,
    out_weight,
):
    size = row_keys.shape[1]
    heads = queries.shape[1] // size
    local_blocks = queries.shape[0] // BLK
    n_x, n_y, n_z = lax.axis_size("x"), lax.axis_size("y"), lax.axis_size("z")
    x, y, core, z = (lax.axis_index(axis) for axis in ("x", "y", "core", "z"))
    rows = doc_ids.shape[0]

    along_z = lambda array, shift: lax.ppermute(array, "z", [(i, (i + shift) % n_z) for i in range(n_z)])

    def pack(keys, values):
        keys, values = keys.reshape(-1, BLK, size), values.reshape(-1, BLK, size)
        return jnp.concatenate([keys, jnp.swapaxes(values, 1, 2)], axis=2)

    packed = jnp.concatenate([pack(row_keys, row_values), pack(cached_keys, cached_values)], axis=0)
    gathered = lax.all_gather(packed, CTX, axis=0, tiled=True)
    columns = out_weight.shape[1] // n_z
    weight_for = lambda shift: lax.dynamic_slice_in_dim(out_weight, ((z + shift) % n_z) * columns, columns, 1)
    weight = jnp.concatenate([weight_for(0)] + [along_z(weight_for(s), s) for s in (1, -1, 2)], axis=0)

    shards = n_x * n_y * 2
    row_base = block_order.reshape(shards, local_blocks) * BLK
    cached_base = rows + jnp.arange(shards, dtype=jnp.int32)[:, None] * BLK
    stage_bases = [jnp.concatenate([row_base, cached_base], axis=1).reshape(-1)]
    shard = (x * n_y + y) * 2 + core
    mine = lax.dynamic_slice_in_dim(block_order, shard * local_blocks, local_blocks, 0)
    stages, bounds = plan(doc_ids, prefix_lens, block_order, mine, stage_bases, heads)
    qt = jnp.transpose(queries.reshape(local_blocks, BLK, heads, size), (0, 3, 2, 1))
    qt = qt.reshape(local_blocks, size, heads * BLK)
    gathered, weight, qt, stages, bounds = lax.optimization_barrier((gathered, weight, qt, stages, bounds))
    part_blocks = local_blocks // 2
    part_rows = part_blocks * BLK
    outs = []
    for part in range(2):
        mine = attend(
            qt,
            (gathered,),
            stages[0],
            bounds,
            None,
            rows,
            "attend_part",
            begin=part * part_blocks,
            blocks=part_blocks,
            last_stage=True,
        )
        below, above = along_z(mine, 1), along_z(mine, -1)
        opposite = jnp.concatenate(
            [along_z(below[: part_rows // 2], 1), along_z(above[part_rows // 2 :], -1)], axis=0
        )
        every = jnp.concatenate([mine, below, above, opposite], axis=1)
        outs.append(jnp.dot(every, weight, preferred_element_type=jnp.float32).astype(jnp.bfloat16))
    return jnp.concatenate(outs, axis=0)


def solution(mesh):
    grid = Mesh(mesh.devices.reshape(4, 4, 2, mesh.shape["head"]), ("x", "y", "core", "z"))
    placed = (
        P(CTX, "z"),
        P(CTX, None),
        P(CTX, None),
        P(CTX, None),
        P(CTX, None),
        P(),
        P(),
        P(),
        P("z", None),
    )
    return jax.shard_map(
        on_device, mesh=grid, in_specs=placed, out_specs=P(CTX, "z"), check_vma=False
    )
```

time: 219 us -> 171 us (0.78); the launches traced: 222 us -> 170 us
  waiting for transfers between devices: 134 us -> 74.4 us
  starting transfers between devices: 6 us -> 15.9 us
  other arithmetic: 8.14 us -> 12.9 us
  matrix products: 9.27 us -> 4.66 us
  local copies, waits for them, and re-layouts: 14.8 us -> 12.1 us
    all_gather x2 -> x1, waiting for transfers between devices: 91.8 us -> 23.1 us  [on_device(): gathered = lax.all_gather(packed, CTX, axis=0, tiled=True)]
    ppermute x0 -> x11, waiting for transfers between devices: none -> 51.3 us  [on_device(): lax.ppermute(array, 'z', [(i, (i + shift) % n_z) for i in range(n_z)])]
    all_to_all x1 -> x0, waiting for transfers between devices: 42 us -> none  [on_device(): weight = lax.all_to_all(out_weight, 'head', 1, 0, tiled=True)]
    ppermute x0 -> x11, starting transfers between devices: none -> 15.9 us  [on_device(): lax.ppermute(array, 'z', [(i, (i + shift) % n_z) for i in range(n_z)])]
    all_to_all x1 -> x0, local copies, waits for them, and re-layouts: 6.58 us -> none  [on_device(): weight = lax.all_to_all(out_weight, 'head', 1, 0, tiled=True)]
    all_to_all x1 -> x0, starting transfers between devices: 5.99 us -> none  [on_device(): weight = lax.all_to_all(out_weight, 'head', 1, 0, tiled=True)]
    unnamed x9 -> x17, local copies, waits for them, and re-layouts: 6.5 us -> 0.91 us
    dot_general x1 -> x2, matrix products: 9.27 us -> 4.66 us  [on_device(): jnp.dot(every, weight, preferred_element_type=jnp.float32)]
  transfers between devices with their start and end apart: 3 -> 12, of which waited for: 3 -> 7; matrix products, arithmetic and copies ran while one was open for 9% -> 12% of each run, Pallas kernels for 0% -> 11%
where the time goes in v2:
time: 171 us; the launch traced here: 170 us
  waiting for transfers between devices  74.4 us (44%)
  Pallas kernels  36.8 us (22%)
  starting transfers between devices  15.9 us (9%)
  between operations  13.8 us (8%)
  other arithmetic  12.9 us (8%)
  local copies, waits for them, and re-layouts  12.1 us (7%)
  matrix products  4.66 us (3%)
    ppermute x11, waiting for transfers between devices, on_device(): lax.ppermute(array, 'z', [(i, (i + shift) % n_z) for i in range(n_z)])  51.3 us
    pallas_call x2, Pallas kernels, attend(): pl.pallas_call(functools.partial(attend_kernel, scale, row_span, first_st...  36.8 us
    all_gather x1, waiting for transfers between devices, on_device(): gathered = lax.all_gather(packed, CTX, axis=0, tiled=True)  23.1 us
    ppermute x11, starting transfers between devices, on_device(): lax.ppermute(array, 'z', [(i, (i + shift) % n_z) for i in range(n_z)])  15.9 us
    dot_general x2, matrix products, on_device(): jnp.dot(every, weight, preferred_element_type=jnp.float32)  4.66 us
    dynamic_slice x1, local copies, waits for them, and re-layouts, on_device(): lax.dynamic_slice_in_dim(out_weight, (z + shift) % n_z * columns, columns...  4.03 us
    sort x1, other arithmetic, plan(): order = lax.sort(key, dimension=2) % 1024  3.94 us
    concatenate x1, other arithmetic, on_device(): jnp.concatenate([weight_for(0)] + [along_z(weight_for(s), s) for s in (1,...  3.69 us
  transfers between devices with their start and end apart: 12, of which 7 were waited for; matrix products, arithmetic and copies ran while one was open for 12% of the time, Pallas kernels for 11%

profile of v2, /device:TPU:1, one launch (start us, length us, event | category | flops | bytes accessed | tf_op | source)
XLA Modules:
  0.0 170.4 jit_solution(13173011691158282053)
XLA Ops:
  6.5 1.1 copy.37
  7.7 0.9 copy.38
  8.5 1.9 %maximum_maximum_fusion = bf16[9,128,256]{2,1,0:T(8,128)(2,1)} fusion(bf16[1,128,128]{2,1,0:T(8,128)(2,1)S(1)} %bitcast.32, bf16[1,128,128]{2,1,0:T(8,128)(2,1)} %bitcast.34, bf16[8,128,128]{2,1,0:T(8,128)(2,1)S(1)} %bitcast.28, bf16[8,128,128]{2,1,0:T(8,128)(2,1)} %bitcast.30), kind=kLoop, calls=%fused_computation.27 | loop fusion | flops 2359296 | bytes 1179648 | tf_op jit(solution)/shard_map/concatenate | solution.py:268
  10.6 4.0 %constant_dynamic-slice_fusion.3 = (bf16[512,1024]{1,0:T(8,128)(2,1)S(1)}, bf16[512,1024]{1,0:T(8,128)(2,1)}, bf16[512,1024]{1,0:T(8,128)(2,1)}, bf16[512,1024]{1,0:T(8,128)(2,1)}) fusion(bf16[512,4096]{1,0:T(8,128)(2,1)} %param.17, s32[]{:T(128)S(6)} %select_n.109, s32[]{:T(128)S(6)} %select_n.111, s32[]{:T(128)S(6)} %select_n.115, s32[]{:T(128)S(6)} %select_n.113), kind=kLoop, calls=%fused_computation.65 | loop fusion | bytes 8388624 | tf_op jit(solution)/shard_map/dynamic_slice | solution.py:271
  14.6 2.5 %collective-permute-start = (bf16[512,1024]{1,0:T(8,128)(2,1)}, bf16[512,1024]{1,0:T(8,128)(2,1)}, u32[]{:S(2)}, u32[]{:S(2)}) collective-permute-start(bf16[512,1024]{1,0:T(8,128)(2,1)} %get-tuple-element.36), channel_id=1, source_target_pairs={{0,1},{1,2},{2,3},{3,0},{4,5},{5,6},{6,7},{7,4},{8,9},{9,10},{10,1... | collective-permute-start | bytes 3145736 | tf_op jit(solution)/shard_map/ppermute | solution.py:262
  17.1 2.1 %collective-permute-start.1 = (bf16[512,1024]{1,0:T(8,128)(2,1)}, bf16[512,1024]{1,0:T(8,128)(2,1)}, u32[]{:S(2)}, u32[]{:S(2)}) collective-permute-start(bf16[512,1024]{1,0:T(8,128)(2,1)} %get-tuple-element.38), channel_id=1, source_target_pairs={{0,3},{1,0},{2,1},{3,2},{4,7},{5,4},{6,5},{7,6},{8,11},{9,8},{10,9... | collective-permute-start | bytes 3145736 | tf_op jit(solution)/shard_map/ppermute | solution.py:262
  19.2 1.3 collective-permute-start.2
  20.5 0.1 copy.40
  20.6 0.1 reduce.2
  20.8 0.1 mul.54
  20.9 0.1 pad_add_fusion
  20.9 0.1 broadcast_in_dim_stack.3.refs_2_
  21.1 0.1 compare_select_fusion
  21.2 0.6 gather_fusion
  21.7 0.5 convert_reduce_fusion
  22.2 0.1 select_reduce_fusion.2
  22.4 0.2 slice_reduce_fusion.2
  22.6 0.2 slice_reduce_fusion.1
  22.7 0.2 slice_reduce_fusion
  23.1 0.7 tile.10.refs_3_
  23.8 0.3 reshape.1195
  24.1 1.7 copy.39
  25.8 1.2 reshape.1196.refs_4_
  27.0 0.2 convert_reduce_fusion.1
  27.2 3.9 %sort.14 = (s32[1,8,288]{2,1,0:T(8,128)S(1)}, s32[1,8,288]{2,1,0:T(8,128)}) sort(s32[1,8,288]{2,1,0:T(8,128)S(1)} %select_select_fusion, s32[1,8,288]{2,1,0:T(8,128)S(1)} %iota.37), dimensions={2}, to_apply=%region_5.6 | sort | flops 27648 | bytes 36864 | tf_op jit(solution)/shard_map/sort | solution.py:239
  31.2 0.6 fusion.27.refs_0_
  31.8 10.6 %collective-permute-done = bf16[512,1024]{1,0:T(8,128)(2,1)} collective-permute-done((bf16[512,1024]{1,0:T(8,128)(2,1)}, bf16[512,1024]{1,0:T(8,128)(2,1)}, u32[]{:S(2)}, u32[]{:S(2)}) %collective-permute-start) | collective-permute-done | bytes 1048608 | tf_op jit(solution)/shard_map/ppermute | solution.py:262
  42.4 23.3 %collective-permute-done.2 = bf16[512,1024]{1,0:T(8,128)(2,1)} collective-permute-done((bf16[512,1024]{1,0:T(8,128)(2,1)}, bf16[512,1024]{1,0:T(8,128)(2,1)}, u32[]{:S(2)}, u32[]{:S(2)}) %collective-permute-start.2) | collective-permute-done | bytes 1048608 | tf_op jit(solution)/shard_map/ppermute | solution.py:262
  65.7 3.7 %pad_maximum_fusion = bf16[2048,1024]{1,0:T(8,128)(2,1)} fusion(bf16[512,1024]{1,0:T(8,128)(2,1)} %collective-permute-done.2, bf16[512,1024]{1,0:T(8,128)(2,1)} %collective-permute-done.1, bf16[512,1024]{1,0:T(8,128)(2,1)} %collective-permute-done, bf16[512,1024]{1,0:T(8,128)(2,1)S(1)} %get-tuple-element.35), kind=kLoop, calls=%fused_computation.1 | loop fusion | flops 16777216 | bytes 8388608 | tf_op jit(solution)/shard_map/concatenate | solution.py:272
  69.4 23.1 %all-gather.2.cloned.1.call-done.refs_5_ = bf16[288,128,256]{2,1,0:T(8,128)(2,1)} async-done(((bf16[9,128,256]{2,1,0:T(8,128)(2,1)}), bf16[288,128,256]{2,1,0:T(8,128)(2,1)}) %all-gather.2.cloned.1.call-update) | async-done | bytes 18874384 | tf_op jit(solution)/shard_map/all_gather | solution.py:269
  92.5 0.7 copy.42.refs_1_
  93.1 17.8 %attend_part.2 = bf16[512,512]{1,0:T(8,128)(2,1)} custom-call(s32[8,288]{1,0:T(8,128)} %fusion.27.refs_0_, s32[8,2]{1,0:T(8,128)} %copy.42.refs_1_, s32[288]{0:T(512)} %copy-done.5, s32[8,8,512]{2,1,0:T(8,128)} %tile.10.refs_3_, bf16[8,128,512]{2,1,0:T(8,128)(2,1)} %reshape.1196.refs_4_, bf16[288,128,256]{2,1,0:T(8,128)(2,1)} %all-gather.2.cloned.1.call-done.refs_5_), custom_call_target="tpu_custom_call" | custom-call | flops 2147483648 | bytes 8388608 | tf_op jit(solution)/shard_map/attend_part/pallas_call | solution.py:181
  111.0 1.3 collective-permute-start.3
  112.3 1.5 collective-permute-start.4
  113.8 18.9 %attend_part.3 = bf16[512,512]{1,0:T(8,128)(2,1)} custom-call(s32[8,288]{1,0:T(8,128)} %fusion.27.refs_0_, s32[8,2]{1,0:T(8,128)} %copy.42.refs_1_, s32[288]{0:T(512)} %copy-done.5, s32[8,8,512]{2,1,0:T(8,128)} %tile.10.refs_3_, bf16[8,128,512]{2,1,0:T(8,128)(2,1)} %reshape.1196.refs_4_, bf16[288,128,256]{2,1,0:T(8,128)(2,1)} %all-gather.2.cloned.1.call-done.refs_5_), custom_call_target="tpu_custom_call" | custom-call | flops 2147483648 | bytes 8388608 | tf_op jit(solution)/shard_map/attend_part/pallas_call | solution.py:181
  132.8 1.5 collective-permute-start.8
  134.2 0.1 collective-permute-start.7
  134.3 0.1 collective-permute-start.5
  134.4 2.7 %collective-permute-start.6 = (bf16[256,512]{1,0:T(8,128)(2,1)S(1)}, bf16[256,512]{1,0:T(8,128)(2,1)S(1)}, u32[]{:S(2)}, u32[]{:S(2)}) collective-permute-start(bf16[256,512]{1,0:T(8,128)(2,1)S(1)} %slice.53), channel_id=1, source_target_pairs={{0,3},{1,0},{2,1},{3,2},{4,7},{5,4},{6,5},{7,6},{8,11},{9,8},{10,9... | collective-permute-start | bytes 786440 | tf_op jit(solution)/shard_map/ppermute | solution.py:262
  137.2 9.2 %collective-permute-done.8 = bf16[512,512]{1,0:T(8,128)(2,1)S(1)} collective-permute-done((bf16[512,512]{1,0:T(8,128)(2,1)}, bf16[512,512]{1,0:T(8,128)(2,1)S(1)}, u32[]{:S(2)}, u32[]{:S(2)}) %collective-permute-start.8) | collective-permute-done | bytes 524320 | tf_op jit(solution)/shard_map/ppermute | solution.py:262
  146.4 2.6 %collective-permute-start.10 = (bf16[256,512]{1,0:T(8,128)(2,1)S(1)}, bf16[256,512]{1,0:T(8,128)(2,1)S(1)}, u32[]{:S(2)}, u32[]{:S(2)}) collective-permute-start(bf16[256,512]{1,0:T(8,128)(2,1)S(1)} %slice.55), channel_id=1, source_target_pairs={{0,3},{1,0},{2,1},{3,2},{4,7},{5,4},{6,5},{7,6},{8,11},{9,8},{10,9... | collective-permute-start | bytes 786440 | tf_op jit(solution)/shard_map/ppermute | solution.py:262
  149.0 0.3 collective-permute-start.9
  149.2 4.9 %collective-permute-done.5 = bf16[256,512]{1,0:T(8,128)(2,1)S(1)} collective-permute-done((bf16[256,512]{1,0:T(8,128)(2,1)S(1)}, bf16[256,512]{1,0:T(8,128)(2,1)S(1)}, u32[]{:S(2)}, u32[]{:S(2)}) %collective-permute-start.5) | collective-permute-done | bytes 262176 | tf_op jit(solution)/shard_map/ppermute | solution.py:262
  154.2 2.3 %fusion.23 = bf16[512,1024]{1,0:T(8,128)(2,1)S(1)} fusion(bf16[2048,1024]{1,0:T(8,128)(2,1)S(1)} %copy-done, bf16[256,512]{1,0:T(8,128)(2,1)S(1)} %collective-permute-done.6, bf16[256,512]{1,0:T(8,128)(2,1)S(1)} %collective-permute-done.5, bf16[512,512]{1,0:T(8,128)(2,1)S(1)} %collective-permute-done.4, bf16[512,512]{1,0:T(8,128)(2,1)S(1)} %collective-permute-done.3, ...), kind=kOutput, calls=%fused_computation.26 | convolution fusion | flops 2158493696 | bytes 7340032 | tf_op jit(solution)/shard_map/dot_general | solution.py:305
  156.5 1.1 collective-permute-done.10
  157.6 2.2 %collective-permute-done.9 = bf16[256,512]{1,0:T(8,128)(2,1)S(1)} collective-permute-done((bf16[256,512]{1,0:T(8,128)(2,1)S(1)}, bf16[256,512]{1,0:T(8,128)(2,1)S(1)}, u32[]{:S(2)}, u32[]{:S(2)}) %collective-permute-start.9) | collective-permute-done | bytes 262176 | tf_op jit(solution)/shard_map/ppermute | solution.py:262
  159.8 2.3 %fusion.20 = bf16[512,1024]{1,0:T(8,128)(2,1)S(1)} fusion(bf16[2048,1024]{1,0:T(8,128)(2,1)S(1)} %copy-done, bf16[256,512]{1,0:T(8,128)(2,1)S(1)} %collective-permute-done.10, bf16[256,512]{1,0:T(8,128)(2,1)S(1)} %collective-permute-done.9, bf16[512,512]{1,0:T(8,128)(2,1)S(1)} %collective-permute-done.8, bf16[512,512]{1,0:T(8,128)(2,1)S(1)} %collective-permute-done.7, ...), kind=kOutput, calls=%fused_computation.25 | convolution fusion | flops 2158493696 | bytes 7340032 | tf_op jit(solution)/shard_map/dot_general | solution.py:305
  162.1 1.5 pad_maximum_fusion.1
  (45 shorter events, 0.4 us)
Async XLA Ops:
  6.5 85.9 %all-gather.2.cloned.1.call-start = ((), (), s32[]{:S(2)}) async-start(), calls=%async_computation | async-start | bytes 19464192 | tf_op jit(solution)/shard_map/all_gather | solution.py:269
  10.5 10.0 %copy-start.7 = (s32[32]{0:T(128)S(1)}, s32[32]{0:T(128)}, u32[]{:S(2)}) copy-start(s32[32]{0:T(128)} %param.15) | copy-start | bytes 388
  10.5 10.2 %copy-start.6 = (s32[256]{0:T(256)S(1)}, s32[256]{0:T(256)}, u32[]{:S(2)}) copy-start(s32[256]{0:T(256)} %param.16) | copy-start | bytes 3076
  10.5 10.6 %copy-start.4 = (s32[32768]{0:T(1024)S(1)}, s32[32768]{0:T(1024)}, u32[]{:S(2)}) copy-start(s32[32768]{0:T(1024)} %param.14) | copy-start | bytes 393220
  10.5 13.3 %copy-start.1 = (bf16[1024,512]{1,0:T(8,128)(2,1)S(1)}, bf16[1024,512]{1,0:T(8,128)(2,1)}, u32[]{:S(2)}) copy-start(bf16[1024,512]{1,0:T(8,128)(2,1)} %param.9) | copy-start | bytes 3145732
  14.6 27.8 %collective-permute-start = (bf16[512,1024]{1,0:T(8,128)(2,1)}, bf16[512,1024]{1,0:T(8,128)(2,1)}, u32[]{:S(2)}, u32[]{:S(2)}) collective-permute-start(bf16[512,1024]{1,0:T(8,128)(2,1)} %get-tuple-element.36), channel_id=1, source_target_pairs={{0,1},{1,2},{2,3},{3,0},{4,5},{5,6},{6,7},{7,4},{8,9},{9,10},{10,1... | collective-permute-start | bytes 3145736 | tf_op jit(solution)/shard_map/ppermute | solution.py:262
  17.1 25.3 %collective-permute-start.1 = (bf16[512,1024]{1,0:T(8,128)(2,1)}, bf16[512,1024]{1,0:T(8,128)(2,1)}, u32[]{:S(2)}, u32[]{:S(2)}) collective-permute-start(bf16[512,1024]{1,0:T(8,128)(2,1)} %get-tuple-element.38), channel_id=1, source_target_pairs={{0,3},{1,0},{2,1},{3,2},{4,7},{5,4},{6,5},{7,6},{8,11},{9,8},{10,9... | collective-permute-start | bytes 3145736 | tf_op jit(solution)/shard_map/ppermute | solution.py:262
  19.2 46.5 %collective-permute-start.2 = (bf16[512,1024]{1,0:T(8,128)(2,1)}, bf16[512,1024]{1,0:T(8,128)(2,1)}, u32[]{:S(2)}, u32[]{:S(2)}) collective-permute-start(bf16[512,1024]{1,0:T(8,128)(2,1)} %get-tuple-element.37), channel_id=1, source_target_pairs={{0,2},{1,3},{2,0},{3,1},{4,6},{5,7},{6,4},{7,5},{8,10},{9,11},{10,... | collective-permute-start | bytes 3145736 | tf_op jit(solution)/shard_map/ppermute | solution.py:262
  21.1 48.3 %copy-start.5 = (s32[288]{0:T(512)}, s32[288]{0:T(512)S(1)}, u32[]{:S(2)}) copy-start(s32[288]{0:T(512)S(1)} %broadcast_in_dim_stack.3.refs_2_) | copy-start | bytes 3460
  111.0 43.2 %copy-start = (bf16[2048,1024]{1,0:T(8,128)(2,1)S(1)}, bf16[2048,1024]{1,0:T(8,128)(2,1)}, u32[]{:S(2)}) copy-start(bf16[2048,1024]{1,0:T(8,128)(2,1)} %pad_maximum_fusion) | copy-start | bytes 12582916
  111.0 43.2 %copy-start.3 = (bf16[512,512]{1,0:T(8,128)(2,1)S(1)}, bf16[512,512]{1,0:T(8,128)(2,1)}, u32[]{:S(2)}) copy-start(bf16[512,512]{1,0:T(8,128)(2,1)} %attend_part.2) | copy-start | bytes 1572868
  111.0 23.3 %collective-permute-start.3 = (bf16[512,512]{1,0:T(8,128)(2,1)}, bf16[512,512]{1,0:T(8,128)(2,1)S(1)}, u32[]{:S(2)}, u32[]{:S(2)}) collective-permute-start(bf16[512,512]{1,0:T(8,128)(2,1)} %attend_part.2), channel_id=1, source_target_pairs={{0,1},{1,2},{2,3},{3,0},{4,5},{5,6},{6,7},{7,4},{8,9},{9,10},{10,1... | collective-permute-start | bytes 1572872 | tf_op jit(solution)/shard_map/ppermute | solution.py:262
  112.3 22.1 %collective-permute-start.4 = (bf16[512,512]{1,0:T(8,128)(2,1)}, bf16[512,512]{1,0:T(8,128)(2,1)S(1)}, u32[]{:S(2)}, u32[]{:S(2)}) collective-permute-start(bf16[512,512]{1,0:T(8,128)(2,1)} %attend_part.2), channel_id=1, source_target_pairs={{0,3},{1,0},{2,1},{3,2},{4,7},{5,4},{6,5},{7,6},{8,11},{9,8},{10,9... | collective-permute-start | bytes 1572872 | tf_op jit(solution)/shard_map/ppermute | solution.py:262
  132.8 13.6 %collective-permute-start.8 = (bf16[512,512]{1,0:T(8,128)(2,1)}, bf16[512,512]{1,0:T(8,128)(2,1)S(1)}, u32[]{:S(2)}, u32[]{:S(2)}) collective-permute-start(bf16[512,512]{1,0:T(8,128)(2,1)} %attend_part.3), channel_id=1, source_target_pairs={{0,3},{1,0},{2,1},{3,2},{4,7},{5,4},{6,5},{7,6},{8,11},{9,8},{10,9... | collective-permute-start | bytes 1572872 | tf_op jit(solution)/shard_map/ppermute | solution.py:262
  134.2 14.7 %collective-permute-start.7 = (bf16[512,512]{1,0:T(8,128)(2,1)}, bf16[512,512]{1,0:T(8,128)(2,1)S(1)}, u32[]{:S(2)}, u32[]{:S(2)}) collective-permute-start(bf16[512,512]{1,0:T(8,128)(2,1)} %attend_part.3), channel_id=1, source_target_pairs={{0,1},{1,2},{2,3},{3,0},{4,5},{5,6},{6,7},{7,4},{8,9},{9,10},{10,1... | collective-permute-start | bytes 1572872 | tf_op jit(solution)/shard_map/ppermute | solution.py:262
  134.3 19.8 %collective-permute-start.5 = (bf16[256,512]{1,0:T(8,128)(2,1)S(1)}, bf16[256,512]{1,0:T(8,128)(2,1)S(1)}, u32[]{:S(2)}, u32[]{:S(2)}) collective-permute-start(bf16[256,512]{1,0:T(8,128)(2,1)S(1)} %slice.52), channel_id=1, source_target_pairs={{0,1},{1,2},{2,3},{3,0},{4,5},{5,6},{6,7},{7,4},{8,9},{9,10},{10,1... | collective-permute-start | bytes 786440 | tf_op jit(solution)/shard_map/ppermute | solution.py:262
  134.4 19.7 %collective-permute-start.6 = (bf16[256,512]{1,0:T(8,128)(2,1)S(1)}, bf16[256,512]{1,0:T(8,128)(2,1)S(1)}, u32[]{:S(2)}, u32[]{:S(2)}) collective-permute-start(bf16[256,512]{1,0:T(8,128)(2,1)S(1)} %slice.53), channel_id=1, source_target_pairs={{0,3},{1,0},{2,1},{3,2},{4,7},{5,4},{6,5},{7,6},{8,11},{9,8},{10,9... | collective-permute-start | bytes 786440 | tf_op jit(solution)/shard_map/ppermute | solution.py:262
  146.4 11.2 %collective-permute-start.10 = (bf16[256,512]{1,0:T(8,128)(2,1)S(1)}, bf16[256,512]{1,0:T(8,128)(2,1)S(1)}, u32[]{:S(2)}, u32[]{:S(2)}) collective-permute-start(bf16[256,512]{1,0:T(8,128)(2,1)S(1)} %slice.55), channel_id=1, source_target_pairs={{0,3},{1,0},{2,1},{3,2},{4,7},{5,4},{6,5},{7,6},{8,11},{9,8},{10,9... | collective-permute-start | bytes 786440 | tf_op jit(solution)/shard_map/ppermute | solution.py:262
  149.0 10.8 %copy-start.2 = (bf16[512,512]{1,0:T(8,128)(2,1)S(1)}, bf16[512,512]{1,0:T(8,128)(2,1)}, u32[]{:S(2)}) copy-start(bf16[512,512]{1,0:T(8,128)(2,1)} %attend_part.3) | copy-start | bytes 1572868
  149.0 10.8 %collective-permute-start.9 = (bf16[256,512]{1,0:T(8,128)(2,1)S(1)}, bf16[256,512]{1,0:T(8,128)(2,1)S(1)}, u32[]{:S(2)}, u32[]{:S(2)}) collective-permute-start(bf16[256,512]{1,0:T(8,128)(2,1)S(1)} %slice.54), channel_id=1, source_target_pairs={{0,1},{1,2},{2,3},{3,0},{4,5},{5,6},{6,7},{7,4},{8,9},{9,10},{10,1... | collective-permute-start | bytes 786440 | tf_op jit(solution)/shard_map/ppermute | solution.py:262
Sparse Core Ops, SparseCore 0:
  10.6 81.8 all-gather.1

commit v3 on v2

v3 whole, which is shorter than its diff:
```python
import functools

import jax
import jax.numpy as jnp
from jax import lax
from jax.experimental import pallas as pl
from jax.experimental.pallas import tpu as pltpu
from jax.sharding import Mesh
from jax.sharding import PartitionSpec as P

BLK = 128
TILE = 4
UNSEEN = -2e30
LOWEST = -1e30
FAR = 1 << 24
CTX = ("x", "y", "core")


def pack_kernel(row_keys, row_values, cached_keys, cached_values, out_ref):
    size = row_keys.shape[1]
    blocks = row_keys.shape[0] // BLK
    for n in range(blocks + 1):
        keys, values = (row_keys, row_values) if n < blocks else (cached_keys, cached_values)
        rows = slice(n * BLK, (n + 1) * BLK) if n < blocks else slice(0, BLK)
        out_ref[n, :, :size] = keys[rows]
        out_ref[n, :, size:] = values[rows].T


def turn_kernel(size, q_ref, qt_ref):
    for j in range(qt_ref.shape[0]):
        for h in range(qt_ref.shape[2] // BLK):
            piece = q_ref[j * BLK : (j + 1) * BLK, h * size : (h + 1) * size]
            qt_ref[j, :, h * BLK : (h + 1) * BLK] = piece.T


def attend_kernel(scale, row_span, shape, stage, first_stage, last_stage, begin, blocks, pieces, *refs):
    table_hbm, bounds_hbm, qt_hbm = refs[:3]
    refs = refs[3:]
    piece_refs, refs = refs[:pieces], refs[pieces:]
    if not first_stage:
        acc_in, top_in, *refs = refs
    if last_stage:
        out_ref, *refs = refs
    else:
        acc_out, top_out, *refs = refs
    table, bounds_ref, qt_ref, kv_ref, acc_ref, top_ref, score_a, score_b, tile_row, tile_first, tile_kind, sems = refs
    size = qt_ref.shape[1]
    wide = qt_ref.shape[2]
    half = wide // 2
    heads = wide // BLK
    depth = TILE * BLK
    span = acc_ref.shape[1]
    total, width, many = shape
    counts_at = total * width
    bases_at = counts_at + total * many

    copies = [pltpu.make_async_copy(table_hbm, table, sems.at[0])]
    at = 0
    for piece in piece_refs:
        target = kv_ref.at[pl.ds(at, piece.shape[0])]
        copies.append(pltpu.make_async_copy(piece, target, sems.at[len(copies)]))
        at += piece.shape[0]
    copies.append(pltpu.make_async_copy(bounds_hbm, bounds_ref, sems.at[len(copies)]))
    copies.append(pltpu.make_async_copy(qt_hbm, qt_ref, sems.at[len(copies)]))
    if not first_stage:
        copies.append(pltpu.make_async_copy(acc_in.at[pl.ds(begin, blocks)], acc_ref, sems.at[len(copies)]))
        copies.append(pltpu.make_async_copy(top_in.at[pl.ds(begin, blocks)], top_ref, sems.at[len(copies)]))
    for copy in copies:
        copy.start()
    if first_stage:
        acc_ref[...] = jnp.zeros(acc_ref.shape, jnp.float32)
        top_ref[...] = jnp.full(top_ref.shape, LOWEST, jnp.float32)

    copies[0].wait()

    def list_row(j, t):
        here = counts_at + (begin + j) * many + 3 * stage
        offset, whole, seen = table[here], table[here + 1], table[here + 2]
        offset = offset + (begin + j) * width

        def list_tile(i, t):
            tile_row[t] = j
            tile_first[t] = offset + i * TILE
            tile_kind[t] = jnp.where(i * TILE + TILE <= whole, TILE + 1, jnp.minimum(seen - i * TILE, TILE))
            return t + 1

        return lax.fori_loop(0, (seen + (TILE - 1)) // TILE, list_tile, t)

    tiles = lax.fori_loop(0, blocks, list_row, 0)
    for n in range(2):
        tile_row[tiles + n] = 0
        tile_first[tiles + n] = 0
        tile_kind[tiles + n] = 0
    for copy in copies[1:]:
        copy.wait()

    ones = jnp.ones((span - size, depth), jnp.bfloat16)
    key_row = lax.broadcasted_iota(jnp.int32, (BLK, half), 0)

    def indices(t):
        first, kind = tile_first[t], tile_kind[t]
        return [jnp.where(n < kind, table[first + n], 0) for n in range(TILE)]

    def score(t, score_ref):
        keys = jnp.concatenate([kv_ref[index & 255, :, :size] for index in indices(t)], axis=0)
        j = tile_row[t] + begin
        for part in range(2):
            cols = slice(part * half, (part + 1) * half)
            score_ref[:, cols] = jnp.dot(keys, qt_ref[j, :, cols], preferred_element_type=jnp.float32)

    def fold(t, score_ref, masked):
        picked = indices(t)
        values = jnp.concatenate([kv_ref[index & 255, :, size:] for index in picked], axis=1)
        values = jnp.concatenate([values, ones], axis=0)
        j = tile_row[t]
        kind = tile_kind[t]
        for part in range(2):
            cols = slice(part * half, (part + 1) * half)
            if masked:
                shown = []
                for n, index in enumerate(picked):
                    base = jnp.where(n < kind, table[bases_at + (index >> 8)], FAR)
                    cached = base >= row_span
                    low = jnp.where(cached, bounds_ref[begin + j, 2:3, cols], bounds_ref[begin + j, 0:1, cols])
                    high = jnp.where(cached, bounds_ref[begin + j, 3:4, cols], bounds_ref[begin + j, 1:2, cols])
                    piece = score_ref[n * BLK : (n + 1) * BLK, cols]
                    shown.append(jnp.where((key_row >= low - base) & (key_row <= high - base), piece, UNSEEN))
                scores = jnp.concatenate(shown, axis=0)
            else:
                scores = score_ref[:, cols]
            old = top_ref[j, 0:1, cols]
            new = jnp.maximum(old, jnp.max(scores, axis=0, keepdims=True))
            weight = jnp.exp2(scores * scale - new * scale).astype(jnp.bfloat16)
            factor = jnp.exp2((old - new) * scale)
            top_ref[j, 0:1, cols] = new
            acc_ref[j, :, cols] = acc_ref[j, :, cols] * factor + jnp.dot(
                values, weight, preferred_element_type=jnp.float32
            )

    def step(t, here, there):
        plain = tile_kind[t] > TILE

        @pl.when(plain)
        def _():
            score(t + 1, there)
            fold(t, here, False)

        @pl.when(jnp.logical_not(plain))
        def _():
            score(t + 1, there)
            fold(t, here, True)

    def pair(i, _):
        step(2 * i, score_a, score_b)
        step(2 * i + 1, score_b, score_a)
        return 0

    @pl.when(tiles > 0)
    def _():
        score(0, score_a)
        lax.fori_loop(0, (tiles + 1) // 2, pair, 0)

    if last_stage:

        def finish(j, _):
            rows = pl.ds(pl.multiple_of(j * BLK, BLK), BLK)
            for h in range(heads):
                cols = slice(h * BLK, (h + 1) * BLK)
                result = acc_ref[j, :size, cols] / acc_ref[j, size : size + 1, cols]
                out_ref[rows, h * size : (h + 1) * size] = result.T.astype(out_ref.dtype)
            return 0

        lax.fori_loop(0, blocks, finish, 0)
    else:
        back = [
            pltpu.make_async_copy(acc_ref, acc_out, sems.at[0]),
            pltpu.make_async_copy(top_ref, top_out, sems.at[1]),
        ]
        for copy in back:
            copy.start()
        for copy in back:
            copy.wait()


def attend(qt, pieces, lists, stage, state, row_span, name, begin=0, blocks=None, last_stage=False):
    table, bounds, shape = lists
    total, size, wide = qt.shape
    blocks = total if blocks is None else blocks
    first_stage = state is None
    scale = 1.4426950408889634 / size**0.5
    span = size + 16
    vmem = pl.BlockSpec(memory_space=pltpu.VMEM)
    hbm = pl.BlockSpec(memory_space=pl.ANY)
    held = sum(piece.shape[0] for piece in pieces)
    tiles = blocks * (held // TILE) + 2
    if last_stage:
        out_shape = jax.ShapeDtypeStruct((blocks * BLK, wide // BLK * size), jnp.bfloat16)
        out_specs = vmem
    else:
        out_shape = (
            jax.ShapeDtypeStruct((total, span, wide), jnp.float32),
            jax.ShapeDtypeStruct((total, 8, wide), jnp.float32),
        )
        out_specs = (hbm, hbm)
    return pl.pallas_call(
        functools.partial(
            attend_kernel, scale, row_span, shape, stage, first_stage, last_stage, begin, blocks, len(pieces)
        ),
        out_shape=out_shape,
        in_specs=[hbm] * (3 + len(pieces) + (0 if first_stage else 2)),
        out_specs=out_specs,
        scratch_shapes=[
            pltpu.SMEM(table.shape, jnp.int32),
            pltpu.VMEM(bounds.shape, jnp.int32),
            pltpu.VMEM(qt.shape, jnp.bfloat16),
            pltpu.VMEM((held, BLK, 2 * size), jnp.bfloat16),
            pltpu.VMEM((blocks, span, wide), jnp.float32),
            pltpu.VMEM((blocks, 8, wide), jnp.float32),
            pltpu.VMEM((TILE * BLK, wide), jnp.float32),
            pltpu.VMEM((TILE * BLK, wide), jnp.float32),
            pltpu.SMEM((tiles,), jnp.int32),
            pltpu.SMEM((tiles,), jnp.int32),
            pltpu.SMEM((tiles,), jnp.int32),
            pltpu.SemaphoreType.DMA((len(pieces) + 5,)),
        ],
        compiler_params=pltpu.CompilerParams(vmem_limit_bytes=56 << 20),
        cost_estimate=pl.CostEstimate(flops=8 << 30, bytes_accessed=16 << 20, transcendentals=8 << 20),
        name=name,
    )(table, bounds, qt, *pieces, *(() if first_stage else state))


def plan(doc_ids, prefix_lens, block_order, mine, stage_of, place_of, heads):
    block_count = block_order.shape[0]
    rows = doc_ids.shape[0]
    shards = stage_of.shape[0]
    stages = 2
    inside = jnp.arange(BLK, dtype=jnp.int32)
    doc = doc_ids.reshape(block_count, BLK)[mine]
    position = mine[:, None] * BLK + inside[None, :]
    docs = jnp.arange(prefix_lens.shape[0], dtype=jnp.int32)
    doc_start = jnp.sum((doc_ids[None, :] < docs[:, None]).astype(jnp.int32), axis=1)
    prefix_end = jnp.cumsum(prefix_lens)
    prefix_start = prefix_end - prefix_lens
    chosen = doc[:, :, None] == docs[None, None, :]
    pick = lambda table: jnp.sum(jnp.where(chosen, table[None, None, :], 0), axis=2)
    low_row, high_row = pick(doc_start), position
    low_cached, high_cached = pick(prefix_start) + rows, pick(prefix_end) + (rows - 1)
    bounds = jnp.stack([low_row, high_row, low_cached, high_cached], axis=1)
    bounds = jnp.tile(bounds, (1, 2, heads)).astype(jnp.int32)
    row_base = block_order.reshape(shards, -1) * BLK
    cached_base = rows + jnp.arange(shards, dtype=jnp.int32)[:, None] * BLK
    base = jnp.concatenate([row_base, cached_base], axis=1).reshape(-1)
    first = base[None, :]
    last = first + (BLK - 1)
    cached = first >= rows
    ends = lambda array, at: array[:, at][:, None]
    seen = jnp.where(
        cached,
        (last >= ends(low_cached, 0)) & (first <= ends(high_cached, -1)),
        (last >= ends(low_row, 0)) & (first <= ends(high_row, -1)),
    )
    whole = jnp.where(
        cached,
        (first >= ends(low_cached, -1)) & (last <= ends(high_cached, 0)),
        (first >= ends(low_row, -1)) & (last <= ends(high_row, 0)),
    )
    unit = base.shape[0] // shards
    index = jnp.arange(base.shape[0], dtype=jnp.int32)
    spread = lambda array: jnp.broadcast_to(array[:, None], (shards, unit)).reshape(-1)
    stage = spread(stage_of)[None, :]
    slot = index * 256 + spread(place_of) * unit + index % unit
    key = jnp.where(seen, stage * (1 << 20) + jnp.where(whole, 0, 1 << 19) + slot[None, :], (1 << 24) + slot[None, :])
    order = lax.sort(key, dimension=1) & ((1 << 19) - 1)
    order = jnp.pad(order, ((0, 0), (0, TILE)))
    counts = []
    offset = jnp.zeros((mine.shape[0],), jnp.int32)
    for n in range(stages):
        here = stage == n
        many = jnp.sum(seen & here, axis=1).astype(jnp.int32)
        counts += [offset, jnp.sum(whole & seen & here, axis=1).astype(jnp.int32), many]
        offset = offset + many
    counts = jnp.stack(counts, axis=1)
    table = jnp.concatenate([order.reshape(-1), counts.reshape(-1), base])
    return table, bounds, (mine.shape[0], order.shape[1], counts.shape[1])


def around(first_axis, shift, n_x, n_y):
    pairs = []
    for x in range(n_x):
        for y in range(n_y):
            for core in range(2):
                along_x = (core == 0) == first_axis
                to = ((x + shift) % n_x, y) if along_x else (x, (y + shift) % n_y)
                pairs.append(((x * n_y + y) * 2 + core, (to[0] * n_y + to[1]) * 2 + core))
    return pairs


def on_device(
    queries,
    row_keys,
    row_values,
    cached_keys,
    cached_values,
    doc_ids,
    prefix_lens,
    block_order,
    out_weight,
):
    size = row_keys.shape[1]
    heads = queries.shape[1] // size
    local_blocks = queries.shape[0] // BLK
    n_x, n_y, n_z = lax.axis_size("x"), lax.axis_size("y"), lax.axis_size("z")
    x, y, core, z = (lax.axis_index(axis) for axis in ("x", "y", "core", "z"))
    rows = doc_ids.shape[0]
    shards = n_x * n_y * 2

    move = lambda array, first_axis, shift: lax.ppermute(array, CTX, around(first_axis, shift, n_x, n_y))
    swap = lambda array: lax.ppermute(array, "core", [(0, 1), (1, 0)])
    along_z = lambda array, shift: lax.ppermute(array, "z", [(i, (i + shift) % n_z) for i in range(n_z)])

    own = pl.pallas_call(
        pack_kernel,
        out_shape=jax.ShapeDtypeStruct((local_blocks + 1, BLK, 2 * size), jnp.bfloat16),
        cost_estimate=pl.CostEstimate(flops=0, bytes_accessed=4 << 20, transcendentals=0),
        name="pack",
    )(row_keys, row_values, cached_keys, cached_values)
    own, out_weight = lax.optimization_barrier((own, out_weight))
    right, left, far = move(own, True, 1), move(own, True, -1), move(own, True, 2)

    columns = out_weight.shape[1] // n_z
    depth = out_weight.shape[0]
    share = depth // 2
    half_for = lambda shift: lax.dynamic_slice(
        out_weight, (core * share, ((z + shift) % n_z) * columns), (share, columns)
    )
    given = [half_for(s) for s in (1, -1, 2)]
    got = [along_z(given[0], 1), along_z(given[1], -1)]
    one = jnp.concatenate([own, right], axis=0)
    one, got, left, far = lax.optimization_barrier((one, got, left, far))
    two = jnp.concatenate([left, far], axis=0)
    near = (move(one, False, 1), move(two, False, -1))
    next_near = (move(two, False, 1), move(one, False, -1))
    two, doc_ids, prefix_lens, block_order, queries = lax.optimization_barrier(
        (two, doc_ids, prefix_lens, block_order, queries)
    )

    shard = jnp.arange(shards, dtype=jnp.int32)
    shard_x, shard_y, shard_core = shard // (2 * n_y), shard // 2 % n_y, shard % 2
    apart_x, apart_y = (x - shard_x) % n_x, (y - shard_y) % n_y
    apart_first = jnp.where(shard_core == 0, apart_x, apart_y)
    apart_second = jnp.where(shard_core == 0, apart_y, apart_x)
    early = apart_first <= 1
    late = jnp.logical_not(early)
    same, facing = apart_second == 0, apart_second == 2
    soon = same | ((apart_second == 1) & early) | ((apart_second == 3) & late)
    stage_of = jnp.where(soon, 0, 1)
    piece_of = jnp.where(same, 0, 2) + late.astype(jnp.int32)
    piece_of = jnp.where(soon | facing, piece_of, early.astype(jnp.int32))
    along = jnp.where(early, apart_first, 3 - apart_first)
    place_of = jnp.where(shard_core == core, 0, 8) + 2 * piece_of + along
    mine = lax.dynamic_slice_in_dim(block_order, ((x * n_y + y) * 2 + core) * local_blocks, local_blocks, 0)
    table, bounds, shape = plan(doc_ids, prefix_lens, block_order, mine, stage_of, place_of, heads)
    qt = pl.pallas_call(
        functools.partial(turn_kernel, size),
        out_shape=jax.ShapeDtypeStruct((local_blocks, size, heads * BLK), jnp.bfloat16),
        cost_estimate=pl.CostEstimate(flops=0, bytes_accessed=4 << 20, transcendentals=0),
        name="turn",
    )(queries)

    lists = (table, bounds, shape)
    both = lambda arrays: tuple(arrays) + tuple(swap(array) for array in arrays)
    swapped = (swap(one), swap(two))
    near, swapped, qt, table, bounds = lax.optimization_barrier((near, swapped, qt, table, bounds))
    lists = (table, bounds, shape)
    across = (move(near[0], False, 1), move(near[1], False, -1))
    near_swapped = tuple(swap(array) for array in near)
    got = got + [along_z(given[2], 2)]
    state = attend(qt, (one, two) + near + swapped + near_swapped, lists, 0, None, rows, "attend_first")
    next_near, across, state, got = lax.optimization_barrier((next_near, across, state, got))
    final = next_near + across + tuple(swap(array) for array in next_near + across)
    part_blocks = local_blocks // 2
    part_rows = part_blocks * BLK
    parts = []
    for part in range(2):
        parts.append(
            attend(
                qt,
                final,
                lists,
                1,
                state,
                rows,
                "attend_last",
                begin=part * part_blocks,
                blocks=part_blocks,
                last_stage=True,
            )
        )
        if part == 0:
            first, state = lax.optimization_barrier((parts[0], state))
            parts[0] = first
    below, above = [along_z(parts[0], 1)], [along_z(parts[0], -1)]
    parts[1], below[0], above[0], got, out_weight = lax.optimization_barrier(
        (parts[1], below[0], above[0], got, out_weight)
    )
    below.append(along_z(parts[1], 1))
    above.append(along_z(parts[1], -1))
    got = jnp.concatenate(got, axis=0)
    other = swap(got)
    weight = jnp.zeros((n_z * depth, columns), out_weight.dtype)
    put = lambda array, piece, row: lax.dynamic_update_slice(array, piece, (row, 0))
    weight = put(weight, lax.dynamic_slice_in_dim(out_weight, z * columns, columns, 1), 0)
    for n in range(3):
        part = slice(n * share, (n + 1) * share)
        weight = put(weight, got[part], (n + 1) * depth + core * share)
        weight = put(weight, other[part], (n + 1) * depth + (1 - core) * share)
    below[1], above[1], weight = lax.optimization_barrier((below[1], above[1], weight))
    known = jnp.concatenate(
        [jnp.concatenate([parts[n], below[n], above[n]], axis=1) for n in range(2)], axis=0
    )
    partial = jnp.dot(known, weight[: 3 * depth], preferred_element_type=jnp.float32)
    opposite = jnp.concatenate([along_z(below[0], 1), along_z(above[1], -1)], axis=0)
    opposite, partial = lax.optimization_barrier((opposite, partial))
    rest = jnp.dot(opposite, weight[3 * depth :], preferred_element_type=jnp.float32)
    return (partial + rest).astype(jnp.bfloat16)


def solution(mesh):
    grid = Mesh(mesh.devices.reshape(4, 4, 2, mesh.shape["head"]), ("x", "y", "core", "z"))
    placed = (
        P(CTX, "z"),
        P(CTX, None),
        P(CTX, None),
        P(CTX, None),
        P(CTX, None),
        P(),
        P(),
        P(),
        P("z", None),
    )
    return jax.shard_map(
        on_device, mesh=grid, in_specs=placed, out_specs=P(CTX, "z"), check_vma=False
    )
```

time: 171 us -> 150 us (0.88)
  the two profiles are of different devices: /device:TPU:1 before, /device:TPU:24 now
where the time goes in v3:
time: 150 us
  Pallas kernels  45.2 us (30%)
  starting transfers between devices  35.1 us (23%)
  waiting for transfers between devices  32.1 us (21%)
  local copies, waits for them, and re-layouts  20.4 us (14%)
  other arithmetic  11.9 us (8%)
  matrix products  4.67 us (3%)
    pallas_call x3, Pallas kernels, attend(): pl.pallas_call(functools.partial(attend_kernel, scale, row_span, shape, s...  40.7 us
    ppermute x9, waiting for transfers between devices, on_device(): lax.ppermute(array, 'z', [(i, (i + shift) % n_z) for i in range(n_z)])  19.5 us
    ppermute x9, starting transfers between devices, on_device(): lax.ppermute(array, 'z', [(i, (i + shift) % n_z) for i in range(n_z)])  15.5 us
    ppermute x9, starting transfers between devices, on_device(): lax.ppermute(array, CTX, around(first_axis, shift, n_x, n_y))  14.6 us
    ppermute x9, waiting for transfers between devices, on_device(): swap = lambda array: lax.ppermute(array, 'core', [(0, 1), (1, 0)])  6.9 us
    ppermute x9, waiting for transfers between devices, on_device(): lax.ppermute(array, CTX, around(first_axis, shift, n_x, n_y))  5.71 us
    ppermute x9, starting transfers between devices, on_device(): swap = lambda array: lax.ppermute(array, 'core', [(0, 1), (1, 0)])  5.03 us
    unnamed x45, local copies, waits for them, and re-layouts  4.51 us
  transfers between devices with their start and end apart: 27, of which 10 were waited for; matrix products, arithmetic and copies ran while one was open for 17% of the time, Pallas kernels for 22%

profile of v3, /device:TPU:24, one launch (start us, length us, event | category | flops | bytes accessed | tf_op | source)
XLA Modules:
  0.0 150.0 jit_solution(14437210240909968613)
XLA Ops:
  0.0 2.0 %pack.1 = bf16[9,128,256]{2,1,0:T(8,128)(2,1)} custom-call(bf16[1024,128]{1,0:T(8,128)(2,1)} %row_keys.1, bf16[1024,128]{1,0:T(8,128)(2,1)} %row_values.1, bf16[128,128]{1,0:T(8,128)(2,1)} %cached_keys.1, bf16[128,128]{1,0:T(8,128)(2,1)} %cached_values.1), custom_call_target="tpu_custom_call" | custom-call | bytes 4194304 | tf_op jit(solution)/shard_map/pack/pallas_call | solution.py:321
  2.0 1.5 collective-permute-start
  3.5 1.7 %collective-permute-start.3 = (bf16[9,128,256]{2,1,0:T(8,128)(2,1)}, bf16[9,128,256]{2,1,0:T(8,128)(2,1)S(1)}, u32[]{:S(2)}, u32[]{:S(2)}) collective-permute-start(bf16[9,128,256]{2,1,0:T(8,128)(2,1)} %pack.1), channel_id=1, source_target_pairs={{0,96},{4,28},{8,104},{12,4},{16,112},{20,12},{24,120},{28,20},{32... | collective-permute-start | bytes 1769480 | tf_op jit(solution)/shard_map/ppermute | solution.py:317
  5.2 1.8 %collective-permute-start.4 = (bf16[9,128,256]{2,1,0:T(8,128)(2,1)}, bf16[9,128,256]{2,1,0:T(8,128)(2,1)}, u32[]{:S(2)}, u32[]{:S(2)}) collective-permute-start(bf16[9,128,256]{2,1,0:T(8,128)(2,1)} %pack.1), channel_id=1, source_target_pairs={{0,64},{4,20},{8,72},{12,28},{16,80},{20,4},{24,88},{28,12},{32,96... | collective-permute-start | bytes 1769480 | tf_op jit(solution)/shard_map/ppermute | solution.py:317
  7.0 2.6 %fusion.32 = (bf16[256,1024]{1,0:T(8,128)(2,1)}, bf16[256,1024]{1,0:T(8,128)(2,1)}, bf16[256,1024]{1,0:T(8,128)(2,1)}) fusion(bf16[512,4096]{1,0:T(8,128)(2,1)} %param.17, s32[]{:T(128)S(6)} %select_n.222, s32[]{:T(128)S(6)} %select_n.251, s32[]{:T(128)S(6)} %select_n.226, s32[]{:T(128)S(6)} %select_n.224), kind=kLoop, calls=%fused_computation.112 | loop fusion | bytes 3145744 | tf_op jit(solution)/shard_map/dynamic_slice | solution.py:333
  9.6 1.9 %collective-permute-start.1 = (bf16[256,1024]{1,0:T(8,128)(2,1)}, bf16[256,1024]{1,0:T(8,128)(2,1)S(1)}, u32[]{:S(2)}, u32[]{:S(2)}) collective-permute-start(bf16[256,1024]{1,0:T(8,128)(2,1)} %get-tuple-element.117), channel_id=1, source_target_pairs={{0,1},{1,2},{2,3},{3,0},{4,5},{5,6},{6,7},{7,4},{8,9},{9,10},{10,1... | collective-permute-start | bytes 1572872 | tf_op jit(solution)/shard_map/ppermute | solution.py:319
  11.5 2.1 %collective-permute-start.2 = (bf16[256,1024]{1,0:T(8,128)(2,1)}, bf16[256,1024]{1,0:T(8,128)(2,1)S(1)}, u32[]{:S(2)}, u32[]{:S(2)}) collective-permute-start(bf16[256,1024]{1,0:T(8,128)(2,1)} %get-tuple-element.116), channel_id=1, source_target_pairs={{0,3},{1,0},{2,1},{3,2},{4,7},{5,4},{6,5},{7,6},{8,11},{9,8},{10,9... | collective-permute-start | bytes 1572872 | tf_op jit(solution)/shard_map/ppermute | solution.py:319
  16.7 1.2 pad_maximum_fusion.1.refs_3_
  17.9 5.2 %collective-permute-done.1 = bf16[256,1024]{1,0:T(8,128)(2,1)S(1)} collective-permute-done((bf16[256,1024]{1,0:T(8,128)(2,1)}, bf16[256,1024]{1,0:T(8,128)(2,1)S(1)}, u32[]{:S(2)}, u32[]{:S(2)}) %collective-permute-start.1) | collective-permute-done | bytes 524320 | tf_op jit(solution)/shard_map/ppermute | solution.py:319
  23.2 0.9 constant_dynamic-update-slice_fusion.1
  24.0 1.9 %constant_dynamic-update-slice_fusion.refs_4_ = bf16[18,128,256]{2,1,0:T(8,128)(2,1)} fusion(bf16[18,128,256]{2,1,0:T(8,128)(2,1)} %constant_dynamic-update-slice_fusion.1, bf16[9,128,256]{2,1,0:T(8,128)(2,1)} %collective-permute-done.4), kind=kLoop, calls=%fused_computation.42 | loop fusion | bytes 1179648 | tf_op jit(solution)/shard_map/concatenate | solution.py:340
  26.9 1.2 collective-permute-start.6
  28.1 2.1 %collective-permute-start.5 = (bf16[18,128,256]{2,1,0:T(8,128)(2,1)S(1)}, bf16[18,128,256]{2,1,0:T(8,128)(2,1)}, u32[]{:S(2)}, u32[]{:S(2)}) collective-permute-start(bf16[18,128,256]{2,1,0:T(8,128)(2,1)S(1)} %pad_maximum_fusion.1.refs_3_), channel_id=1, source_target_pairs={{0,8},{4,36},{8,16},{12,44},{16,24},{20,52},{24,0},{28,60},{32,40}... | collective-permute-start | bytes 3538952 | tf_op jit(solution)/shard_map/ppermute | solution.py:317
  30.2 0.8 compare_select_fusion
  31.0 0.7 copy.22
  35.0 0.7 tile.10.refs_1_
  35.8 0.8 convert_reduce_fusion.2
  36.9 3.9 %sort.14 = (s32[8,288]{1,0:T(8,128)S(1)}, s32[8,288]{1,0:T(8,128)}) sort(s32[8,288]{1,0:T(8,128)S(1)} %add_select_fusion, s32[8,288]{1,0:T(8,128)S(1)} %iota.50), dimensions={1}, to_apply=%region_5.6 | sort | flops 27648 | bytes 36864 | tf_op jit(solution)/shard_map/sort | solution.py:273
  40.9 2.5 %turn.1.refs_2_ = bf16[8,128,512]{2,1,0:T(8,128)(2,1)} custom-call(bf16[1024,512]{1,0:T(8,128)(2,1)} %q_ref), custom_call_target="tpu_custom_call" | custom-call | bytes 4194304 | tf_op jit(solution)/shard_map/turn/pallas_call | solution.py:363
  45.2 3.0 %collective-permute-start.9 = (bf16[18,128,256]{2,1,0:T(8,128)(2,1)}, bf16[18,128,256]{2,1,0:T(8,128)(2,1)S(1)}, u32[]{:S(2)}, u32[]{:S(2)}) collective-permute-start(bf16[18,128,256]{2,1,0:T(8,128)(2,1)} %constant_dynamic-update-slice_fusion.refs_4_), channel_id=1, source_target_pairs={{0,8},{4,36},{8,16},{12,44},{16,24},{20,52},{24,0},{28,60},{32,40}... | collective-permute-start | bytes 3538952 | tf_op jit(solution)/shard_map/ppermute | solution.py:317
  48.3 3.2 %collective-permute-start.11 = (bf16[18,128,256]{2,1,0:T(8,128)(2,1)}, bf16[18,128,256]{2,1,0:T(8,128)(2,1)S(1)}, u32[]{:S(2)}, u32[]{:S(2)}) collective-permute-start(bf16[18,128,256]{2,1,0:T(8,128)(2,1)} %collective-permute-done.5.refs_5_), channel_id=1, source_target_pairs={{0,8},{4,36},{8,16},{12,44},{16,24},{20,52},{24,0},{28,60},{32,40}... | collective-permute-start | bytes 3538952 | tf_op jit(solution)/shard_map/ppermute | solution.py:317
  51.5 1.0 copy-done.15
  52.5 2.9 %collective-permute-start.15 = (bf16[256,1024]{1,0:T(8,128)(2,1)S(1)}, bf16[256,1024]{1,0:T(8,128)(2,1)S(1)}, u32[]{:S(2)}, u32[]{:S(2)}) collective-permute-start(bf16[256,1024]{1,0:T(8,128)(2,1)S(1)} %copy-done.2), channel_id=1, source_target_pairs={{0,2},{1,3},{2,0},{3,1},{4,6},{5,7},{6,4},{7,5},{8,10},{9,11},{10,... | collective-permute-start | bytes 1572872 | tf_op jit(solution)/shard_map/ppermute | solution.py:319
  55.5 17.7 %attend_first.1 = (f32[8,144,512]{2,1,0:T(8,128)}, f32[8,8,512]{2,1,0:T(8,128)}) custom-call(s32[2672]{0:T(1024)} %concatenate.30.refs_0_, s32[8,8,512]{2,1,0:T(8,128)} %tile.10.refs_1_, bf16[8,128,512]{2,1,0:T(8,128)(2,1)} %turn.1.refs_2_, bf16[18,128,256]{2,1,0:T(8,128)(2,1)} %copy-done.1, bf16[18,128,256]{2,1,0:T(8,128)(2,1)} %constant_dynamic-update-slice_fusion.refs_4_, ...), custom_call_target="tpu_custom_call" | custom-call | flops 8589934592 | bytes 16777216 | tf_op jit(solution)/shard_map/attend_first/pallas_call | solution.py:205
  73.2 1.7 %collective-permute-done.11.refs_5_ = bf16[18,128,256]{2,1,0:T(8,128)(2,1)S(1)} collective-permute-done((bf16[18,128,256]{2,1,0:T(8,128)(2,1)}, bf16[18,128,256]{2,1,0:T(8,128)(2,1)S(1)}, u32[]{:S(2)}, u32[]{:S(2)}) %collective-permute-start.11) | collective-permute-done | bytes 1179680 | tf_op jit(solution)/shard_map/ppermute | solution.py:317
  74.9 3.4 %collective-permute-done.12.refs_6_ = bf16[18,128,256]{2,1,0:T(8,128)(2,1)S(1)} collective-permute-done((bf16[18,128,256]{2,1,0:T(8,128)(2,1)}, bf16[18,128,256]{2,1,0:T(8,128)(2,1)S(1)}, u32[]{:S(2)}, u32[]{:S(2)}) %collective-permute-start.12) | collective-permute-done | bytes 1179680 | tf_op jit(solution)/shard_map/ppermute | solution.py:317
  79.3 1.8 %collective-permute-done.16.refs_7_ = bf16[18,128,256]{2,1,0:T(8,128)(2,1)S(1)} collective-permute-done((bf16[18,128,256]{2,1,0:T(8,128)(2,1)S(1)}, bf16[18,128,256]{2,1,0:T(8,128)(2,1)S(1)}, u32[]{:S(2)}, u32[]{:S(2)}) %collective-permute-start.16) | collective-permute-done | bytes 1179680 | tf_op jit(solution)/shard_map/ppermute | solution.py:318
  81.2 3.4 %collective-permute-done.17.refs_8_ = bf16[18,128,256]{2,1,0:T(8,128)(2,1)S(1)} collective-permute-done((bf16[18,128,256]{2,1,0:T(8,128)(2,1)S(1)}, bf16[18,128,256]{2,1,0:T(8,128)(2,1)S(1)}, u32[]{:S(2)}, u32[]{:S(2)}) %collective-permute-start.17) | collective-permute-done | bytes 1179680 | tf_op jit(solution)/shard_map/ppermute | solution.py:318
  84.5 1.7 %collective-permute-done.18.refs_9_ = bf16[18,128,256]{2,1,0:T(8,128)(2,1)S(1)} collective-permute-done((bf16[18,128,256]{2,1,0:T(8,128)(2,1)S(1)}, bf16[18,128,256]{2,1,0:T(8,128)(2,1)S(1)}, u32[]{:S(2)}, u32[]{:S(2)}) %collective-permute-start.18) | collective-permute-done | bytes 1179680 | tf_op jit(solution)/shard_map/ppermute | solution.py:318
  86.2 1.1 copy-done.14
  87.4 9.8 %attend_last.2 = bf16[512,512]{1,0:T(8,128)(2,1)} custom-call(s32[2672]{0:T(1024)} %concatenate.30.refs_0_, s32[8,8,512]{2,1,0:T(8,128)} %tile.10.refs_1_, bf16[8,128,512]{2,1,0:T(8,128)(2,1)} %turn.1.refs_2_, bf16[18,128,256]{2,1,0:T(8,128)(2,1)} %copy-done.8, bf16[18,128,256]{2,1,0:T(8,128)(2,1)} %copy-done.9, bf16[18,128,256]{2,1,0:T(8,128)(2,1)} %copy-done.10, ...), custom_call_target="tpu_custom_call" | custom-call | flops 8589934592 | bytes 16777216 | tf_op jit(solution)/shard_map/attend_last/pallas_call | solution.py:205
  97.2 1.3 collective-permute-start.20
  98.6 2.0 %collective-permute-start.21 = (bf16[512,512]{1,0:T(8,128)(2,1)}, bf16[512,512]{1,0:T(8,128)(2,1)S(1)}, u32[]{:S(2)}, u32[]{:S(2)}) collective-permute-start(bf16[512,512]{1,0:T(8,128)(2,1)} %attend_last.2), channel_id=1, source_target_pairs={{0,3},{1,0},{2,1},{3,2},{4,7},{5,4},{6,5},{7,6},{8,11},{9,8},{10,9... | collective-permute-start | bytes 1572872 | tf_op jit(solution)/shard_map/ppermute | solution.py:319
  100.5 13.1 %attend_last.3 = bf16[512,512]{1,0:T(8,128)(2,1)} custom-call(s32[2672]{0:T(1024)} %concatenate.30.refs_0_, s32[8,8,512]{2,1,0:T(8,128)} %tile.10.refs_1_, bf16[8,128,512]{2,1,0:T(8,128)(2,1)} %turn.1.refs_2_, bf16[18,128,256]{2,1,0:T(8,128)(2,1)} %copy-done.8, bf16[18,128,256]{2,1,0:T(8,128)(2,1)} %copy-done.9, bf16[18,128,256]{2,1,0:T(8,128)(2,1)} %copy-done.10, ...), custom_call_target="tpu_custom_call" | custom-call | flops 8589934592 | bytes 16777216 | tf_op jit(solution)/shard_map/attend_last/pallas_call | solution.py:205
  113.7 0.8 copy-done.17
  115.3 2.9 %collective-permute-start.25 = (bf16[768,1024]{1,0:T(8,128)(2,1)S(1)}, bf16[768,1024]{1,0:T(8,128)(2,1)}, u32[]{:S(2)}, u32[]{:S(2)}) collective-permute-start(bf16[768,1024]{1,0:T(8,128)(2,1)S(1)} %pad_maximum_fusion), channel_id=1, source_target_pairs={{0,4},{4,0},{1,5},{5,1},{2,6},{6,2},{3,7},{7,3},{8,12},{12,8},{9,1... | collective-permute-start | bytes 4718600 | tf_op jit(solution)/shard_map/ppermute | solution.py:318
  118.2 3.2 %collective-permute-start.24 = (bf16[512,512]{1,0:T(8,128)(2,1)}, bf16[512,512]{1,0:T(8,128)(2,1)S(1)}, u32[]{:S(2)}, u32[]{:S(2)}) collective-permute-start(bf16[512,512]{1,0:T(8,128)(2,1)} %attend_last.3), channel_id=1, source_target_pairs={{0,3},{1,0},{2,1},{3,2},{4,7},{5,4},{6,5},{7,6},{8,11},{9,8},{10,9... | collective-permute-start | bytes 1572872 | tf_op jit(solution)/shard_map/ppermute | solution.py:319
  121.4 1.3 constant_dynamic-slice_fusion
  123.4 1.2 slice_dynamic-update-slice_fusion.2
  124.6 1.1 slice_dynamic-update-slice_fusion.1
  125.8 1.1 slice_dynamic-update-slice_fusion
  126.9 7.5 %collective-permute-done.23 = bf16[512,512]{1,0:T(8,128)(2,1)S(1)} collective-permute-done((bf16[512,512]{1,0:T(8,128)(2,1)}, bf16[512,512]{1,0:T(8,128)(2,1)S(1)}, u32[]{:S(2)}, u32[]{:S(2)}) %collective-permute-start.23) | collective-permute-done | bytes 524320 | tf_op jit(solution)/shard_map/ppermute | solution.py:319
  134.4 2.0 %collective-permute-start.26 = (bf16[512,512]{1,0:T(8,128)(2,1)S(1)}, bf16[512,512]{1,0:T(8,128)(2,1)S(1)}, u32[]{:S(2)}, u32[]{:S(2)}) collective-permute-start(bf16[512,512]{1,0:T(8,128)(2,1)S(1)} %collective-permute-done.24), channel_id=1, source_target_pairs={{0,3},{1,0},{2,1},{3,2},{4,7},{5,4},{6,5},{7,6},{8,11},{9,8},{10,9... | collective-permute-start | bytes 1572872 | tf_op jit(solution)/shard_map/ppermute | solution.py:319
  136.4 3.4 %fusion = f32[1024,1024]{1,0:T(8,128)S(1)} fusion(bf16[512,512]{1,0:T(8,128)(2,1)S(1)} %collective-permute-done.24, bf16[512,512]{1,0:T(8,128)(2,1)S(1)} %collective-permute-done.23, bf16[512,512]{1,0:T(8,128)(2,1)S(1)} %copy-done.21, bf16[512,512]{1,0:T(8,128)(2,1)S(1)} %copy-done.20, bf16[512,512]{1,0:T(8,128)(2,1)S(1)} %copy-done.18, ...), kind=kOutput, calls=%fused_computation.4 | convolution fusion | flops 3240099840 | bytes 10485760 | tf_op jit(solution)/shard_map/dot_general | solution.py:421
  139.8 4.9 %collective-permute-done.22 = bf16[512,512]{1,0:T(8,128)(2,1)S(1)} collective-permute-done((bf16[512,512]{1,0:T(8,128)(2,1)}, bf16[512,512]{1,0:T(8,128)(2,1)S(1)}, u32[]{:S(2)}, u32[]{:S(2)}) %collective-permute-start.22) | collective-permute-done | bytes 524320 | tf_op jit(solution)/shard_map/ppermute | solution.py:319
  144.7 1.9 %collective-permute-done.26 = bf16[512,512]{1,0:T(8,128)(2,1)S(1)} collective-permute-done((bf16[512,512]{1,0:T(8,128)(2,1)S(1)}, bf16[512,512]{1,0:T(8,128)(2,1)S(1)}, u32[]{:S(2)}, u32[]{:S(2)}) %collective-permute-start.26) | collective-permute-done | bytes 524320 | tf_op jit(solution)/shard_map/ppermute | solution.py:319
  146.7 1.3 fusion.13
  147.9 2.0 %add_convert_fusion = bf16[1024,1024]{1,0:T(8,128)(2,1)} fusion(f32[1024,1024]{1,0:T(8,128)S(1)} %fusion, f32[1024,1024]{1,0:T(8,128)S(1)} %fusion.13), kind=kLoop, calls=%fused_computation.1 | loop fusion | flops 2097152 | bytes 10485760 | tf_op jit(solution)/shard_map/convert_element_type | solution.py:425
  (122 shorter events, 12.0 us)
Async XLA Ops:
  2.0 14.7 %copy-start = (bf16[9,128,256]{2,1,0:T(8,128)(2,1)S(1)}, bf16[9,128,256]{2,1,0:T(8,128)(2,1)}, u32[]{:S(2)}) copy-start(bf16[9,128,256]{2,1,0:T(8,128)(2,1)} %pack.1) | copy-start | bytes 1769476
  2.0 14.7 %collective-permute-start = (bf16[9,128,256]{2,1,0:T(8,128)(2,1)}, bf16[9,128,256]{2,1,0:T(8,128)(2,1)}, u32[]{:S(2)}, u32[]{:S(2)}) collective-permute-start(bf16[9,128,256]{2,1,0:T(8,128)(2,1)} %pack.1), channel_id=1, source_target_pairs={{0,32},{4,12},{8,40},{12,20},{16,48},{20,28},{24,56},{28,4},{32,64... | collective-permute-start | bytes 1769480 | tf_op jit(solution)/shard_map/ppermute | solution.py:317
  3.5 19.7 %collective-permute-start.3 = (bf16[9,128,256]{2,1,0:T(8,128)(2,1)}, bf16[9,128,256]{2,1,0:T(8,128)(2,1)S(1)}, u32[]{:S(2)}, u32[]{:S(2)}) collective-permute-start(bf16[9,128,256]{2,1,0:T(8,128)(2,1)} %pack.1), channel_id=1, source_target_pairs={{0,96},{4,28},{8,104},{12,4},{16,112},{20,12},{24,120},{28,20},{32... | collective-permute-start | bytes 1769480 | tf_op jit(solution)/shard_map/ppermute | solution.py:317
  5.2 17.9 %collective-permute-start.4 = (bf16[9,128,256]{2,1,0:T(8,128)(2,1)}, bf16[9,128,256]{2,1,0:T(8,128)(2,1)}, u32[]{:S(2)}, u32[]{:S(2)}) collective-permute-start(bf16[9,128,256]{2,1,0:T(8,128)(2,1)} %pack.1), channel_id=1, source_target_pairs={{0,64},{4,20},{8,72},{12,28},{16,80},{20,4},{24,88},{28,12},{32,96... | collective-permute-start | bytes 1769480 | tf_op jit(solution)/shard_map/ppermute | solution.py:317
  9.6 23.0 %copy-start.3 = (s32[32768]{0:T(1024)S(1)}, s32[32768]{0:T(1024)}, u32[]{:S(2)}) copy-start(s32[32768]{0:T(1024)} %param.14) | copy-start | bytes 393220
  9.6 13.5 %collective-permute-start.1 = (bf16[256,1024]{1,0:T(8,128)(2,1)}, bf16[256,1024]{1,0:T(8,128)(2,1)S(1)}, u32[]{:S(2)}, u32[]{:S(2)}) collective-permute-start(bf16[256,1024]{1,0:T(8,128)(2,1)} %get-tuple-element.117), channel_id=1, source_target_pairs={{0,1},{1,2},{2,3},{3,0},{4,5},{5,6},{6,7},{7,4},{8,9},{9,10},{10,1... | collective-permute-start | bytes 1572872 | tf_op jit(solution)/shard_map/ppermute | solution.py:319
  11.5 11.6 %collective-permute-start.2 = (bf16[256,1024]{1,0:T(8,128)(2,1)}, bf16[256,1024]{1,0:T(8,128)(2,1)S(1)}, u32[]{:S(2)}, u32[]{:S(2)}) collective-permute-start(bf16[256,1024]{1,0:T(8,128)(2,1)} %get-tuple-element.116), channel_id=1, source_target_pairs={{0,3},{1,0},{2,1},{3,2},{4,7},{5,4},{6,5},{7,6},{8,11},{9,8},{10,9... | collective-permute-start | bytes 1572872 | tf_op jit(solution)/shard_map/ppermute | solution.py:319
  17.9 37.6 %copy-start.1 = (bf16[18,128,256]{2,1,0:T(8,128)(2,1)}, bf16[18,128,256]{2,1,0:T(8,128)(2,1)S(1)}, u32[]{:S(2)}) copy-start(bf16[18,128,256]{2,1,0:T(8,128)(2,1)S(1)} %pad_maximum_fusion.1.refs_3_) | copy-start | bytes 3538948
  17.9 17.9 %copy-start.7 = (pred[288]{0:T(512)(128)(4,1)S(1)}, pred[288]{0:T(512)(128)(4,1)}, u32[]{:S(2)}) copy-start(pred[288]{0:T(512)(128)(4,1)} %eq.121) | copy-start | bytes 868
  17.9 18.9 %copy-start.4 = (s32[288]{0:T(512)S(1)}, s32[288]{0:T(512)}, u32[]{:S(2)}) copy-start(s32[288]{0:T(512)} %mul.129) | copy-start | bytes 3460
  17.9 18.9 %copy-start.5 = (s32[288]{0:T(512)S(1)}, s32[288]{0:T(512)}, u32[]{:S(2)}) copy-start(s32[288]{0:T(512)} %get-tuple-element.113) | copy-start | bytes 3460
  17.9 18.9 %copy-start.6 = (s32[288]{0:T(512)S(1)}, s32[288]{0:T(512)}, u32[]{:S(2)}) copy-start(s32[288]{0:T(512)} %get-tuple-element.114) | copy-start | bytes 3460
  17.9 34.6 %copy-start.2 = (bf16[256,1024]{1,0:T(8,128)(2,1)S(1)}, bf16[256,1024]{1,0:T(8,128)(2,1)}, u32[]{:S(2)}) copy-start(bf16[256,1024]{1,0:T(8,128)(2,1)} %get-tuple-element.115) | copy-start | bytes 1572868
  26.9 17.8 %collective-permute-start.6 = (bf16[18,128,256]{2,1,0:T(8,128)(2,1)}, bf16[18,128,256]{2,1,0:T(8,128)(2,1)}, u32[]{:S(2)}, u32[]{:S(2)}) collective-permute-start(bf16[18,128,256]{2,1,0:T(8,128)(2,1)} %constant_dynamic-update-slice_fusion.refs_4_), channel_id=1, source_target_pairs={{0,24},{4,100},{8,0},{12,108},{16,8},{20,116},{24,16},{28,124},{32... | collective-permute-start | bytes 3538952 | tf_op jit(solution)/shard_map/ppermute | solution.py:317
  28.1 16.6 %collective-permute-start.5 = (bf16[18,128,256]{2,1,0:T(8,128)(2,1)S(1)}, bf16[18,128,256]{2,1,0:T(8,128)(2,1)}, u32[]{:S(2)}, u32[]{:S(2)}) collective-permute-start(bf16[18,128,256]{2,1,0:T(8,128)(2,1)S(1)} %pad_maximum_fusion.1.refs_3_), channel_id=1, source_target_pairs={{0,8},{4,36},{8,16},{12,44},{16,24},{20,52},{24,0},{28,60},{32,40}... | collective-permute-start | bytes 3538952 | tf_op jit(solution)/shard_map/ppermute | solution.py:317
  30.2 14.5 %collective-permute-start.7 = (bf16[18,128,256]{2,1,0:T(8,128)(2,1)S(1)}, bf16[18,128,256]{2,1,0:T(8,128)(2,1)}, u32[]{:S(2)}, u32[]{:S(2)}) collective-permute-start(bf16[18,128,256]{2,1,0:T(8,128)(2,1)S(1)} %pad_maximum_fusion.1.refs_3_), channel_id=1, source_target_pairs={{0,4},{4,0},{1,5},{5,1},{2,6},{6,2},{3,7},{7,3},{8,12},{12,8},{9,1... | collective-permute-start | bytes 3538952 | tf_op jit(solution)/shard_map/ppermute | solution.py:318
  34.2 9.9 %collective-permute-start.8 = (bf16[18,128,256]{2,1,0:T(8,128)(2,1)}, bf16[18,128,256]{2,1,0:T(8,128)(2,1)}, u32[]{:S(2)}, u32[]{:S(2)}) collective-permute-start(bf16[18,128,256]{2,1,0:T(8,128)(2,1)} %constant_dynamic-update-slice_fusion.refs_4_), channel_id=1, source_target_pairs={{0,4},{4,0},{1,5},{5,1},{2,6},{6,2},{3,7},{7,3},{8,12},{12,8},{9,1... | collective-permute-start | bytes 3538952 | tf_op jit(solution)/shard_map/ppermute | solution.py:318
  44.7 6.8 %collective-permute-start.13 = (bf16[18,128,256]{2,1,0:T(8,128)(2,1)}, bf16[18,128,256]{2,1,0:T(8,128)(2,1)}, u32[]{:S(2)}, u32[]{:S(2)}) collective-permute-start(bf16[18,128,256]{2,1,0:T(8,128)(2,1)} %collective-permute-done.5.refs_5_), channel_id=1, source_target_pairs={{0,4},{4,0},{1,5},{5,1},{2,6},{6,2},{3,7},{7,3},{8,12},{12,8},{9,1... | collective-permute-start | bytes 3538952 | tf_op jit(solution)/shard_map/ppermute | solution.py:318
  44.7 6.8 %collective-permute-start.14 = (bf16[18,128,256]{2,1,0:T(8,128)(2,1)}, bf16[18,128,256]{2,1,0:T(8,128)(2,1)S(1)}, u32[]{:S(2)}, u32[]{:S(2)}) collective-permute-start(bf16[18,128,256]{2,1,0:T(8,128)(2,1)} %collective-permute-done.6.refs_6_), channel_id=1, source_target_pairs={{0,4},{4,0},{1,5},{5,1},{2,6},{6,2},{3,7},{7,3},{8,12},{12,8},{9,1... | collective-permute-start | bytes 3538952 | tf_op jit(solution)/shard_map/ppermute | solution.py:318
  45.2 27.9 %collective-permute-start.9 = (bf16[18,128,256]{2,1,0:T(8,128)(2,1)}, bf16[18,128,256]{2,1,0:T(8,128)(2,1)S(1)}, u32[]{:S(2)}, u32[]{:S(2)}) collective-permute-start(bf16[18,128,256]{2,1,0:T(8,128)(2,1)} %constant_dynamic-update-slice_fusion.refs_4_), channel_id=1, source_target_pairs={{0,8},{4,36},{8,16},{12,44},{16,24},{20,52},{24,0},{28,60},{32,40}... | collective-permute-start | bytes 3538952 | tf_op jit(solution)/shard_map/ppermute | solution.py:317
  48.3 24.9 %collective-permute-start.10 = (bf16[18,128,256]{2,1,0:T(8,128)(2,1)S(1)}, bf16[18,128,256]{2,1,0:T(8,128)(2,1)S(1)}, u32[]{:S(2)}, u32[]{:S(2)}) collective-permute-start(bf16[18,128,256]{2,1,0:T(8,128)(2,1)S(1)} %pad_maximum_fusion.1.refs_3_), channel_id=1, source_target_pairs={{0,24},{4,100},{8,0},{12,108},{16,8},{20,116},{24,16},{28,124},{32... | collective-permute-start | bytes 3538952 | tf_op jit(solution)/shard_map/ppermute | solution.py:317
  48.3 26.7 %collective-permute-start.11 = (bf16[18,128,256]{2,1,0:T(8,128)(2,1)}, bf16[18,128,256]{2,1,0:T(8,128)(2,1)S(1)}, u32[]{:S(2)}, u32[]{:S(2)}) collective-permute-start(bf16[18,128,256]{2,1,0:T(8,128)(2,1)} %collective-permute-done.5.refs_5_), channel_id=1, source_target_pairs={{0,8},{4,36},{8,16},{12,44},{16,24},{20,52},{24,0},{28,60},{32,40}... | collective-permute-start | bytes 3538952 | tf_op jit(solution)/shard_map/ppermute | solution.py:317
  51.5 26.8 %collective-permute-start.12 = (bf16[18,128,256]{2,1,0:T(8,128)(2,1)}, bf16[18,128,256]{2,1,0:T(8,128)(2,1)S(1)}, u32[]{:S(2)}, u32[]{:S(2)}) collective-permute-start(bf16[18,128,256]{2,1,0:T(8,128)(2,1)} %collective-permute-done.6.refs_6_), channel_id=1, source_target_pairs={{0,24},{4,100},{8,0},{12,108},{16,8},{20,116},{24,16},{28,124},{32... | collective-permute-start | bytes 3538952 | tf_op jit(solution)/shard_map/ppermute | solution.py:317
  51.5 1.0 copy-start.15
  52.5 20.6 %collective-permute-start.15 = (bf16[256,1024]{1,0:T(8,128)(2,1)S(1)}, bf16[256,1024]{1,0:T(8,128)(2,1)S(1)}, u32[]{:S(2)}, u32[]{:S(2)}) collective-permute-start(bf16[256,1024]{1,0:T(8,128)(2,1)S(1)} %copy-done.2), channel_id=1, source_target_pairs={{0,2},{1,3},{2,0},{3,1},{4,6},{5,7},{6,4},{7,5},{8,10},{9,11},{10,... | collective-permute-start | bytes 1572872 | tf_op jit(solution)/shard_map/ppermute | solution.py:319
  73.2 14.2 %copy-start.8 = (bf16[18,128,256]{2,1,0:T(8,128)(2,1)}, bf16[18,128,256]{2,1,0:T(8,128)(2,1)S(1)}, u32[]{:S(2)}) copy-start(bf16[18,128,256]{2,1,0:T(8,128)(2,1)S(1)} %collective-permute-done.9.refs_3_) | copy-start | bytes 3538948
  73.2 14.1 %copy-start.9 = (bf16[18,128,256]{2,1,0:T(8,128)(2,1)}, bf16[18,128,256]{2,1,0:T(8,128)(2,1)S(1)}, u32[]{:S(2)}) copy-start(bf16[18,128,256]{2,1,0:T(8,128)(2,1)S(1)} %collective-permute-done.10.refs_4_) | copy-start | bytes 3538948
  74.9 12.4 %copy-start.10 = (bf16[18,128,256]{2,1,0:T(8,128)(2,1)}, bf16[18,128,256]{2,1,0:T(8,128)(2,1)S(1)}, u32[]{:S(2)}) copy-start(bf16[18,128,256]{2,1,0:T(8,128)(2,1)S(1)} %collective-permute-done.11.refs_5_) | copy-start | bytes 3538948
  78.3 9.0 %copy-start.11 = (bf16[18,128,256]{2,1,0:T(8,128)(2,1)}, bf16[18,128,256]{2,1,0:T(8,128)(2,1)S(1)}, u32[]{:S(2)}) copy-start(bf16[18,128,256]{2,1,0:T(8,128)(2,1)S(1)} %collective-permute-done.12.refs_6_) | copy-start | bytes 3538948
  78.3 2.8 %collective-permute-start.16 = (bf16[18,128,256]{2,1,0:T(8,128)(2,1)S(1)}, bf16[18,128,256]{2,1,0:T(8,128)(2,1)S(1)}, u32[]{:S(2)}, u32[]{:S(2)}) collective-permute-start(bf16[18,128,256]{2,1,0:T(8,128)(2,1)S(1)} %collective-permute-done.9.refs_3_), channel_id=1, source_target_pairs={{0,4},{4,0},{1,5},{5,1},{2,6},{6,2},{3,7},{7,3},{8,12},{12,8},{9,1... | collective-permute-start | bytes 3538952 | tf_op jit(solution)/shard_map/ppermute | solution.py:318
  78.5 6.1 %collective-permute-start.17 = (bf16[18,128,256]{2,1,0:T(8,128)(2,1)S(1)}, bf16[18,128,256]{2,1,0:T(8,128)(2,1)S(1)}, u32[]{:S(2)}, u32[]{:S(2)}) collective-permute-start(bf16[18,128,256]{2,1,0:T(8,128)(2,1)S(1)} %collective-permute-done.10.refs_4_), channel_id=1, source_target_pairs={{0,4},{4,0},{1,5},{5,1},{2,6},{6,2},{3,7},{7,3},{8,12},{12,8},{9,1... | collective-permute-start | bytes 3538952 | tf_op jit(solution)/shard_map/ppermute | solution.py:318
  78.8 7.4 %collective-permute-start.18 = (bf16[18,128,256]{2,1,0:T(8,128)(2,1)S(1)}, bf16[18,128,256]{2,1,0:T(8,128)(2,1)S(1)}, u32[]{:S(2)}, u32[]{:S(2)}) collective-permute-start(bf16[18,128,256]{2,1,0:T(8,128)(2,1)S(1)} %collective-permute-done.11.refs_5_), channel_id=1, source_target_pairs={{0,4},{4,0},{1,5},{5,1},{2,6},{6,2},{3,7},{7,3},{8,12},{12,8},{9,1... | collective-permute-start | bytes 3538952 | tf_op jit(solution)/shard_map/ppermute | solution.py:318
  79.0 8.4 %collective-permute-start.19 = (bf16[18,128,256]{2,1,0:T(8,128)(2,1)S(1)}, bf16[18,128,256]{2,1,0:T(8,128)(2,1)}, u32[]{:S(2)}, u32[]{:S(2)}) collective-permute-start(bf16[18,128,256]{2,1,0:T(8,128)(2,1)S(1)} %collective-permute-done.12.refs_6_), channel_id=1, source_target_pairs={{0,4},{4,0},{1,5},{5,1},{2,6},{6,2},{3,7},{7,3},{8,12},{12,8},{9,1... | collective-permute-start | bytes 3538952 | tf_op jit(solution)/shard_map/ppermute | solution.py:318
  81.2 6.2 %copy-start.12 = (bf16[18,128,256]{2,1,0:T(8,128)(2,1)}, bf16[18,128,256]{2,1,0:T(8,128)(2,1)S(1)}, u32[]{:S(2)}) copy-start(bf16[18,128,256]{2,1,0:T(8,128)(2,1)S(1)} %collective-permute-done.16.refs_7_) | copy-start | bytes 3538948
  84.5 1.7 %copy-start.13 = (bf16[18,128,256]{2,1,0:T(8,128)(2,1)}, bf16[18,128,256]{2,1,0:T(8,128)(2,1)S(1)}, u32[]{:S(2)}) copy-start(bf16[18,128,256]{2,1,0:T(8,128)(2,1)S(1)} %collective-permute-done.17.refs_8_) | copy-start | bytes 3538948
  86.2 1.1 copy-start.14
  97.2 16.4 %collective-permute-start.20 = (bf16[512,512]{1,0:T(8,128)(2,1)}, bf16[512,512]{1,0:T(8,128)(2,1)S(1)}, u32[]{:S(2)}, u32[]{:S(2)}) collective-permute-start(bf16[512,512]{1,0:T(8,128)(2,1)} %attend_last.2), channel_id=1, source_target_pairs={{0,1},{1,2},{2,3},{3,0},{4,5},{5,6},{6,7},{7,4},{8,9},{9,10},{10,1... | collective-permute-start | bytes 1572872 | tf_op jit(solution)/shard_map/ppermute | solution.py:319
  98.6 15.1 %collective-permute-start.21 = (bf16[512,512]{1,0:T(8,128)(2,1)}, bf16[512,512]{1,0:T(8,128)(2,1)S(1)}, u32[]{:S(2)}, u32[]{:S(2)}) collective-permute-start(bf16[512,512]{1,0:T(8,128)(2,1)} %attend_last.2), channel_id=1, source_target_pairs={{0,3},{1,0},{2,1},{3,2},{4,7},{5,4},{6,5},{7,6},{8,11},{9,8},{10,9... | collective-permute-start | bytes 1572872 | tf_op jit(solution)/shard_map/ppermute | solution.py:319
  113.7 0.8 copy-start.17
  115.3 8.1 %collective-permute-start.25 = (bf16[768,1024]{1,0:T(8,128)(2,1)S(1)}, bf16[768,1024]{1,0:T(8,128)(2,1)}, u32[]{:S(2)}, u32[]{:S(2)}) collective-permute-start(bf16[768,1024]{1,0:T(8,128)(2,1)S(1)} %pad_maximum_fusion), channel_id=1, source_target_pairs={{0,4},{4,0},{1,5},{5,1},{2,6},{6,2},{3,7},{7,3},{8,12},{12,8},{9,1... | collective-permute-start | bytes 4718600 | tf_op jit(solution)/shard_map/ppermute | solution.py:318
  118.2 16.2 %collective-permute-start.23 = (bf16[512,512]{1,0:T(8,128)(2,1)}, bf16[512,512]{1,0:T(8,128)(2,1)S(1)}, u32[]{:S(2)}, u32[]{:S(2)}) collective-permute-start(bf16[512,512]{1,0:T(8,128)(2,1)} %attend_last.3), channel_id=1, source_target_pairs={{0,1},{1,2},{2,3},{3,0},{4,5},{5,6},{6,7},{7,4},{8,9},{9,10},{10,1... | collective-permute-start | bytes 1572872 | tf_op jit(solution)/shard_map/ppermute | solution.py:319
  118.2 16.2 %collective-permute-start.24 = (bf16[512,512]{1,0:T(8,128)(2,1)}, bf16[512,512]{1,0:T(8,128)(2,1)S(1)}, u32[]{:S(2)}, u32[]{:S(2)}) collective-permute-start(bf16[512,512]{1,0:T(8,128)(2,1)} %attend_last.3), channel_id=1, source_target_pairs={{0,3},{1,0},{2,1},{3,2},{4,7},{5,4},{6,5},{7,6},{8,11},{9,8},{10,9... | collective-permute-start | bytes 1572872 | tf_op jit(solution)/shard_map/ppermute | solution.py:319
  121.4 23.3 %collective-permute-start.22 = (bf16[512,512]{1,0:T(8,128)(2,1)}, bf16[512,512]{1,0:T(8,128)(2,1)S(1)}, u32[]{:S(2)}, u32[]{:S(2)}) collective-permute-start(bf16[512,512]{1,0:T(8,128)(2,1)} %copy-done.17), channel_id=1, source_target_pairs={{0,1},{1,2},{2,3},{3,0},{4,5},{5,6},{6,7},{7,4},{8,9},{9,10},{10,1... | collective-permute-start | bytes 1572872 | tf_op jit(solution)/shard_map/ppermute | solution.py:319
  123.3 13.2 %copy-start.16 = (bf16[512,512]{1,0:T(8,128)(2,1)S(1)}, bf16[512,512]{1,0:T(8,128)(2,1)}, u32[]{:S(2)}) copy-start(bf16[512,512]{1,0:T(8,128)(2,1)} %attend_last.2) | copy-start | bytes 1572868
  123.3 13.1 %copy-start.18 = (bf16[512,512]{1,0:T(8,128)(2,1)S(1)}, bf16[512,512]{1,0:T(8,128)(2,1)}, u32[]{:S(2)}) copy-start(bf16[512,512]{1,0:T(8,128)(2,1)} %copy-done.17) | copy-start | bytes 1572868
  123.3 13.1 %copy-start.20 = (bf16[512,512]{1,0:T(8,128)(2,1)S(1)}, bf16[512,512]{1,0:T(8,128)(2,1)}, u32[]{:S(2)}) copy-start(bf16[512,512]{1,0:T(8,128)(2,1)} %copy-done.19) | copy-start | bytes 1572868
  123.3 13.1 %copy-start.21 = (bf16[512,512]{1,0:T(8,128)(2,1)S(1)}, bf16[512,512]{1,0:T(8,128)(2,1)}, u32[]{:S(2)}) copy-start(bf16[512,512]{1,0:T(8,128)(2,1)} %attend_last.3) | copy-start | bytes 1572868
  134.4 12.2 %collective-permute-start.26 = (bf16[512,512]{1,0:T(8,128)(2,1)S(1)}, bf16[512,512]{1,0:T(8,128)(2,1)S(1)}, u32[]{:S(2)}, u32[]{:S(2)}) collective-permute-start(bf16[512,512]{1,0:T(8,128)(2,1)S(1)} %collective-permute-done.24), channel_id=1, source_target_pairs={{0,3},{1,0},{2,1},{3,2},{4,7},{5,4},{6,5},{7,6},{8,11},{9,8},{10,9... | collective-permute-start | bytes 1572872 | tf_op jit(solution)/shard_map/ppermute | solution.py:319
  (1 other events, 0.8 us)
